TPU v7x, 128 devices: a whole 4x4x4 slice. The times are simulated.
128 devices in a mesh: dp: 16 (over y, z_lo, core), fsdp: 8 (over z_hi, x).
Axes of the slice: x: 4, y: 4, z: 4 (z_hi: 2, z_lo: 2; z = z_hi * 2 + z_lo), core: 2. Of those that a mesh axis runs over, the one named last changes fastest.
Arguments:
- layer_input: bfloat16 [16384, 8192], P(('dp', 'fsdp')), may hold values from -24 to 24
- queries: bfloat16 [16384, 8192], P(('dp', 'fsdp')), may hold values from -48 to 48
- key_rows: bfloat16 [16384, 1024], P(('dp', 'fsdp')), may hold values from -15 to 15
- grad_out: bfloat16 [16384, 8192], P(('dp', 'fsdp')), may hold values from -6 to 6
- w_value: bfloat16 [8192, 1024], P('fsdp'), may hold values from -0.0625 to 0.0625
- destination: int32 [16384], P(('dp', 'fsdp')), may hold values from 0 to 2047, as said below
- seg_start: int32 [16384], P(('dp', 'fsdp')), may hold values from 0 to 127, as said below
Outputs:
- grad_queries: bfloat16 [16384, 8192], P(('dp', 'fsdp'))
- grad_keys: bfloat16 [16384, 1024], P(('dp', 'fsdp'))
- grad_input: bfloat16 [16384, 8192], P(('dp', 'fsdp'))
- grad_weight: float32 [8192, 1024], P(('dp', 'fsdp'))
Inputs may be any that keep to these rules, and one draw needn't show every extreme that they name: `destination`: within each fsdp index the 2048 tokens map one to one onto the packed rows of the same fsdp index. The tokens of one device go to one dp index in numbers between 6 and 10; 10 is reached by every device. seg_start[r] <= r for the row r of a device, all rows from seg_start[r] to r share it, and row 0 of every device begins a rollout.
All inputs are finite; a program needn't handle non-finite values.
Results may differ from a plain program's by a relative error of at most 0.012.
Values may be sent and summed in bfloat16 or wider, within the bound.
A program may use at most 256 MiB of HBM per device.

v0:
```python
import jax
import jax.numpy as jnp
from jax import lax
from jax.sharding import PartitionSpec as P

HD = 128


def attend(queries, key_rows, value_rows, grad_rows, starts):
    tokens_here = queries.shape[0]
    key_heads = key_rows.shape[1] // HD
    group_size = queries.shape[1] // key_rows.shape[1]
    query_split = queries.reshape(tokens_here, key_heads, group_size, HD)
    grad_split = grad_rows.reshape(tokens_here, key_heads, group_size, HD)
    key_split = key_rows.reshape(tokens_here, key_heads, HD)
    value_split = value_rows.reshape(tokens_here, key_heads, HD)
    inverse_root = 1.0 / HD**0.5
    positions = jnp.arange(tokens_here, dtype=jnp.int32)
    allowed = (positions[None, :] <= positions[:, None]) & (positions[None, :] >= starts[:, None])
    scores = (
        jnp.einsum("ikgd,jkd->kgij", query_split, key_split, preferred_element_type=jnp.float32)
        * inverse_root
    )
    scores = jnp.where(allowed[None, None], scores, -1e30)
    row_peak = jnp.max(scores, axis=-1, keepdims=True)
    exponent = jnp.where(allowed[None, None], jnp.exp(scores - row_peak), 0.0)
    softmax_rows = exponent / jnp.sum(exponent, axis=-1, keepdims=True)
    softmax_low = softmax_rows.astype(jnp.bfloat16)
    outputs = jnp.einsum(
        "kgij,jkd->ikgd", softmax_low, value_split, preferred_element_type=jnp.float32
    )
    grad_probs = jnp.einsum(
        "ikgd,jkd->kgij", grad_split, value_split, preferred_element_type=jnp.float32
    )
    row_dots = jnp.einsum("ikgd,ikgd->kgi", grad_split.astype(jnp.float32), outputs)
    grad_scores = (softmax_rows * (grad_probs - row_dots[..., None])).astype(jnp.bfloat16)
    grad_query = (
        jnp.einsum("kgij,jkd->ikgd", grad_scores, key_split, preferred_element_type=jnp.float32)
        * inverse_root
    ).astype(jnp.bfloat16)
    grad_key = (
        jnp.einsum("kgij,ikgd->jkd", grad_scores, query_split, preferred_element_type=jnp.float32)
        * inverse_root
    ).astype(jnp.bfloat16)
    grad_value = jnp.einsum(
        "kgij,ikgd->jkd", softmax_low, grad_split, preferred_element_type=jnp.float32
    ).astype(jnp.bfloat16)
    return (
        grad_query.reshape(tokens_here, -1),
        grad_key.reshape(tokens_here, -1),
        grad_value.reshape(tokens_here, -1),
    )


def project(layer_input, w_value):
    full_weight = lax.all_gather(w_value, "fsdp", axis=0, tiled=True)
    values = jnp.dot(layer_input, full_weight, preferred_element_type=jnp.float32).astype(
        jnp.bfloat16
    )
    return (full_weight, values)


def shards(layer_input, queries, key_rows, grad_out, w_value, destination, seg_start):
    row_count = layer_input.shape[0]
    rank_count = lax.axis_size("dp")
    even_share = row_count // rank_count
    slot_count = even_share + even_share // 4
    total_slots = rank_count * slot_count
    target = destination // row_count
    target_row = destination % row_count
    onehot = (target[:, None] == jnp.arange(rank_count, dtype=jnp.int32)[None, :]).astype(
        jnp.float32
    )
    positions = jnp.arange(row_count, dtype=jnp.int32)
    earlier = (positions[None, :] < positions[:, None]).astype(jnp.float32)
    before = jnp.dot(earlier, onehot, precision=lax.Precision.HIGHEST)
    order_within = jnp.sum(onehot * before, axis=1).astype(jnp.int32)
    slot_index = target * slot_count + order_within
    selector = slot_index[None, :] == jnp.arange(total_slots, dtype=jnp.int32)[:, None]
    picker = selector.astype(jnp.bfloat16)
    labels = jnp.sum(jnp.where(selector, target_row[None, :] + 1, 0), axis=1)
    upper_part = (labels // 64).astype(jnp.bfloat16).reshape(rank_count, slot_count)
    lower_part = (labels % 64).astype(jnp.bfloat16).reshape(rank_count, slot_count)

    def gather_slots(data):
        return (
            jnp.dot(picker, data, preferred_element_type=jnp.float32)
            .astype(jnp.bfloat16)
            .reshape(rank_count, slot_count, data.shape[1])
        )

    query_send = gather_slots(queries)
    grad_send = gather_slots(grad_out)
    key_send = gather_slots(key_rows)
    full_weight, values = project(layer_input, w_value)
    query_arrived, grad_arrived, key_arrived, value_arrived, upper_arrived, lower_arrived = (
        lax.all_to_all(query_send, "dp", split_axis=0, concat_axis=0, tiled=True),
        lax.all_to_all(grad_send, "dp", split_axis=0, concat_axis=0, tiled=True),
        lax.all_to_all(key_send, "dp", split_axis=0, concat_axis=0, tiled=True),
        lax.all_to_all(gather_slots(values), "dp", split_axis=0, concat_axis=0, tiled=True),
        lax.all_to_all(upper_part, "dp", split_axis=0, concat_axis=0, tiled=True),
        lax.all_to_all(lower_part, "dp", split_axis=0, concat_axis=0, tiled=True),
    )
    arrived = upper_arrived.astype(jnp.float32).reshape(-1) * 64.0 + lower_arrived.astype(
        jnp.float32
    ).reshape(-1)
    placer = (arrived[None, :] == (positions + 1).astype(jnp.float32)[:, None]).astype(jnp.bfloat16)

    def to_rows(received):
        return jnp.dot(
            placer, received.reshape(total_slots, -1), preferred_element_type=jnp.float32
        ).astype(jnp.bfloat16)

    grad_query, grad_key, grad_value = attend(
        to_rows(query_arrived),
        to_rows(key_arrived),
        to_rows(value_arrived),
        to_rows(grad_arrived),
        seg_start,
    )

    def to_slots(data):
        return (
            jnp.einsum("rs,rw->sw", placer, data, preferred_element_type=jnp.float32)
            .astype(jnp.bfloat16)
            .reshape(rank_count, slot_count, data.shape[1])
        )

    query_returned, key_returned, value_returned = (
        lax.all_to_all(to_slots(grad_query), "dp", split_axis=0, concat_axis=0, tiled=True),
        lax.all_to_all(to_slots(grad_key), "dp", split_axis=0, concat_axis=0, tiled=True),
        lax.all_to_all(to_slots(grad_value), "dp", split_axis=0, concat_axis=0, tiled=True),
    )

    def from_slots(received):
        return jnp.einsum(
            "sr,sw->rw",
            picker,
            received.reshape(total_slots, -1),
            preferred_element_type=jnp.float32,
        ).astype(jnp.bfloat16)

    grad_queries = from_slots(query_returned)
    grad_keys = from_slots(key_returned)
    grad_values = from_slots(value_returned)
    grad_input = lax.dot_general(
        grad_values, full_weight, (((1,), (1,)), ((), ())), preferred_element_type=jnp.float32
    ).astype(jnp.bfloat16)
    grad_weight = lax.psum_scatter(
        lax.dot_general(
            layer_input, grad_values, (((0,), (0,)), ((), ())), preferred_element_type=jnp.float32
        ),
        ("dp", "fsdp"),
        scatter_dimension=0,
        tiled=True,
    )
    return (grad_queries, grad_keys, grad_input, grad_weight)


def solution(mesh):
    return jax.shard_map(
        shards,
        mesh=mesh,
        in_specs=(
            P(("dp", "fsdp"), None),
            P(("dp", "fsdp"), None),
            P(("dp", "fsdp"), None),
            P(("dp", "fsdp"), None),
            P("fsdp", None),
            P(("dp", "fsdp")),
            P(("dp", "fsdp")),
        ),
        out_specs=(
            P(("dp", "fsdp"), None),
            P(("dp", "fsdp"), None),
            P(("dp", "fsdp"), None),
            P(("dp", "fsdp"), None),
        ),
        check_vma=False,
    )
```

profile of v0, /device:TPU:1, one launch (start us, length us, event | category | flops | bytes accessed | tf_op | source)
XLA Modules:
  0.0 982.8 jit_solution(14085477139622469613)
XLA Ops:
  8.1 0.7 all-gather.2.cloned.1.call-update
  8.7 0.7 fusion.51
  9.8 0.6 copy.47
  10.4 7.3 all-to-all-start.1
  17.8 0.6 copy.46
  18.4 4.8 all-to-all-done.1
  23.2 3.9 all-to-all-start
  27.1 1.2 convolution_convert_fusion.10
  28.3 0.9 reshape.251
  29.2 3.5 all-to-all-done
  32.7 3.9 all-to-all-start.2
  36.6 4.0 convolution_convert_fusion.1
  40.6 4.8 reshape.260
  45.4 1.0 all-to-all-done.2
  46.4 5.6 all-to-all-start.5
  51.9 3.9 convolution_convert_fusion.2
  55.9 4.7 reshape.254
  60.6 44.4 %all-to-all-done.5 = bf16[16,10,8192]{2,1,0:T(8,128)(2,1)} async-done(((bf16[16,10,8192]{2,1,0:T(8,128)(2,1)}), bf16[16,10,8192]{2,1,0:T(8,128)(2,1)}, u32[]{:S(2)}, u32[]{:S(2)}) %all-to-all-start.5) | async-done | bytes 2621472 | tf_op jit(solution)/shard_map/all_to_all | solution.py:98
  105.0 11.1 %all-to-all-start.3 = ((bf16[16,10,8192]{2,1,0:T(8,128)(2,1)}), bf16[16,10,8192]{2,1,0:T(8,128)(2,1)}, u32[]{:S(2)}, u32[]{:S(2)}) async-start(bf16[16,10,8192]{2,1,0:T(8,128)(2,1)} %reshape.254), calls=%async_computation.3 | async-start | bytes 8388608 | tf_op jit(solution)/shard_map/all_to_all | solution.py:97
  117.1 4.8 reshape.261
  121.9 2.5 fusion.13
  124.4 1.9 copy.84
  126.3 49.2 %all-to-all-done.3 = bf16[16,10,8192]{2,1,0:T(8,128)(2,1)} async-done(((bf16[16,10,8192]{2,1,0:T(8,128)(2,1)}), bf16[16,10,8192]{2,1,0:T(8,128)(2,1)}, u32[]{:S(2)}, u32[]{:S(2)}) %all-to-all-start.3) | async-done | bytes 2621472 | tf_op jit(solution)/shard_map/all_to_all | solution.py:97
  175.5 4.7 reshape.255
  180.2 2.5 fusion.12
  182.8 0.6 copy.82
  183.4 1.3 copy-done.2
  184.7 1.7 fusion.6
  186.4 1.2 fusion.54
  187.6 2.0 copy-done.3
  189.6 1.9 fusion.11
  191.5 4.1 copy.57
  195.7 3.3 fusion.16
  199.0 0.3 convolution_convert_fusion.7
  199.5 14.8 %all_to_all.47 = bf16[16,10,1024]{2,1,0:T(8,128)(2,1)} all-to-all(bf16[16,10,1024]{2,1,0:T(8,128)(2,1)S(1)} %reshape.270), channel_id=1, replica_groups=mesh['dp'=16,'fsdp'=8] {'dp'}, dimensions={0} | all-to-all | bytes 655360 | tf_op jit(solution)/shard_map/all_to_all | solution.py:132
  214.2 1.2 reshape.271
  215.7 13.1 %convolution_bitcast_fusion = f32[8192,1024]{0,1:T(8,128)} fusion(bf16[128,1024]{1,0:T(8,128)(2,1)S(1)} %convolution_convert_fusion.11, bf16[128,8192]{1,0:T(8,128)(2,1)S(1)} %copy-done), kind=kOutput, calls=%fused_computation.1 | convolution fusion | flops 2147483648 | bytes 35913728 | tf_op jit(solution)/shard_map/dot_general | solution.py:150
  228.8 33.6 %copy.79 = f32[8192,1024]{1,0:T(8,128)} copy(f32[8192,1024]{0,1:T(8,128)} %convolution_bitcast_fusion) | data formatting | bytes 67108864
  262.4 21.3 %all-gather.2.cloned.1.call-done = bf16[8192,1024]{1,0:T(8,128)(2,1)} async-done(((bf16[1024,1024]{1,0:T(8,128)(2,1)}), bf16[8192,1024]{1,0:T(8,128)(2,1)}) %all-gather.2.cloned.1.call-update) | async-done | bytes 16777232 | tf_op jit(solution)/shard_map/all_gather | solution.py:56
  283.7 8.4 convolution_convert_fusion.9
  292.1 0.9 reshape.257
  293.0 7.6 all-to-all-start.4
  300.6 4.0 bitcast_convert_fusion
  304.6 5.5 copy.68
  310.1 4.4 all-to-all-done.4
  315.3 3.7 fusion.1
  319.0 1.0 copy-done.4
  320.0 3.1 fusion.3
  323.1 4.1 copy.56
  327.2 3.3 fusion.15
  330.5 0.3 convolution_convert_fusion.8
  330.9 0.9 reshape.267
  331.8 7.2 all-to-all-start.7
  339.0 2.3 multiply_convert_fusion
  341.3 2.4 convolution_convert_fusion
  343.8 4.7 reshape.264
  348.5 5.9 all-to-all-done.7
  354.4 4.8 all-to-all-start.6
  359.2 12.8 %convolution_convert_fusion.3 = bf16[128,8192]{1,0:T(8,128)(2,1)} fusion(bf16[128,1024]{1,0:T(8,128)(2,1)S(1)} %convolution_convert_fusion.11, bf16[8192,1024]{1,0:T(8,128)(2,1)} %all-gather.2.cloned.1.call-done), kind=kOutput, calls=%fused_computation.5 | convolution fusion | flops 2148532224 | bytes 19136512 | tf_op jit(solution)/shard_map/dot_general | solution.py:146
  372.1 1.0 convolution_convert_fusion.12
  373.1 72.3 %all-to-all-done.6 = bf16[16,10,8192]{2,1,0:T(8,128)(2,1)} async-done(((bf16[16,10,8192]{2,1,0:T(8,128)(2,1)}), bf16[16,10,8192]{2,1,0:T(8,128)(2,1)}, u32[]{:S(2)}, u32[]{:S(2)}) %all-to-all-start.6) | async-done | bytes 2621472 | tf_op jit(solution)/shard_map/all_to_all | solution.py:130
  445.4 4.8 reshape.265
  450.1 3.8 convolution_convert_fusion.4
  454.0 521.4 %reduce-scatter.4.cloned.1.call-done = f32[64,1024]{1,0:T(8,128)} async-done(((f32[8192,1024]{1,0:T(8,128)}), f32[64,1024]{1,0:T(8,128)}) %reduce-scatter.4.cloned.1.call-update) | async-done | bytes 262160
  (32 shorter events, 2.7 us)
Async XLA Ops:
  8.0 207.7 %copy-start = (bf16[128,8192]{1,0:T(8,128)(2,1)S(1)}, bf16[128,8192]{1,0:T(8,128)(2,1)}, u32[]{:S(2)}) copy-start(bf16[128,8192]{1,0:T(8,128)(2,1)} %param.7) | copy-start | bytes 6291460
  8.0 275.7 %all-gather.2.cloned.1.call-start = ((), (), s32[]{:S(2)}) async-start(), calls=%async_computation.10 | async-start | bytes 18874368 | tf_op jit(solution)/shard_map/all_gather | solution.py:56
  10.4 12.8 %all-to-all-start.1 = ((bf16[16,1,10]{2,1,0:T(2,128)(2,1)}), bf16[16,1,10]{2,1,0:T(2,128)(2,1)S(1)}, u32[]{:S(2)}, u32[]{:S(2)}) async-start(bf16[16,1,10]{2,1,0:T(2,128)(2,1)} %copy.47), calls=%async_computation.1 | async-start | bytes 16384 | tf_op jit(solution)/shard_map/all_to_all | solution.py:102
  23.2 9.5 all-to-all-start
  32.7 13.7 %all-to-all-start.2 = ((bf16[16,10,1024]{2,1,0:T(8,128)(2,1)}), bf16[16,10,1024]{2,1,0:T(8,128)(2,1)S(1)}, u32[]{:S(2)}, u32[]{:S(2)}) async-start(bf16[16,10,1024]{2,1,0:T(8,128)(2,1)} %reshape.251), calls=%async_computation.2 | async-start | bytes 1048576 | tf_op jit(solution)/shard_map/all_to_all | solution.py:99
  46.4 58.6 %all-to-all-start.5 = ((bf16[16,10,8192]{2,1,0:T(8,128)(2,1)}), bf16[16,10,8192]{2,1,0:T(8,128)(2,1)}, u32[]{:S(2)}, u32[]{:S(2)}) async-start(bf16[16,10,8192]{2,1,0:T(8,128)(2,1)} %reshape.260), calls=%async_computation.5 | async-start | bytes 8388608 | tf_op jit(solution)/shard_map/all_to_all | solution.py:98
  60.6 55.7 %copy-start.5 = (s32[128]{0:T(128)S(1)}, s32[128]{0:T(128)}, u32[]{:S(2)}) copy-start(s32[128]{0:T(128)} %param.13) | copy-start | bytes 1540
  105.0 70.5 %all-to-all-start.3 = ((bf16[16,10,8192]{2,1,0:T(8,128)(2,1)}), bf16[16,10,8192]{2,1,0:T(8,128)(2,1)}, u32[]{:S(2)}, u32[]{:S(2)}) async-start(bf16[16,10,8192]{2,1,0:T(8,128)(2,1)} %reshape.254), calls=%async_computation.3 | async-start | bytes 8388608 | tf_op jit(solution)/shard_map/all_to_all | solution.py:97
  116.0 859.3 %reduce-scatter.4.cloned.1.call-start = ((), (), s32[]{:S(2)}) async-start(), calls=%async_computation.11 | async-start | bytes 33816576
  183.4 1.3 copy-start.2
  187.6 2.0 copy-start.3
  293.0 21.6 %all-to-all-start.4 = ((bf16[16,10,1024]{2,1,0:T(8,128)(2,1)}), bf16[16,10,1024]{2,1,0:T(8,128)(2,1)S(1)}, u32[]{:S(2)}, u32[]{:S(2)}) async-start(bf16[16,10,1024]{2,1,0:T(8,128)(2,1)} %reshape.257), calls=%async_computation.4 | async-start | bytes 1048576 | tf_op jit(solution)/shard_map/all_to_all | solution.py:100
  315.2 3.8 copy-start.1
  315.2 4.7 copy-start.4
  331.8 22.6 %all-to-all-start.7 = ((bf16[16,10,1024]{2,1,0:T(8,128)(2,1)}), bf16[16,10,1024]{2,1,0:T(8,128)(2,1)S(1)}, u32[]{:S(2)}, u32[]{:S(2)}) async-start(bf16[16,10,1024]{2,1,0:T(8,128)(2,1)} %reshape.267), calls=%async_computation.7 | async-start | bytes 1048576 | tf_op jit(solution)/shard_map/all_to_all | solution.py:131
  354.4 91.0 %all-to-all-start.6 = ((bf16[16,10,8192]{2,1,0:T(8,128)(2,1)}), bf16[16,10,8192]{2,1,0:T(8,128)(2,1)}, u32[]{:S(2)}, u32[]{:S(2)}) async-start(bf16[16,10,8192]{2,1,0:T(8,128)(2,1)} %reshape.264), calls=%async_computation.6 | async-start | bytes 8388608 | tf_op jit(solution)/shard_map/all_to_all | solution.py:130
Sparse Core Ops, SparseCore 0:
  11.2 272.4 all-gather.1
Sparse Core Ops, SparseCore 1:
  262.5 712.9 reduce-scatter.3
where the time goes:
time: 999 us; the launch traced here: 983 us
  waiting for transfers between devices  729 us (73%)
  local copies, waits for them, and re-layouts  88.9 us (9%)
  matrix products  74.7 us (7%)
  starting transfers between devices  51.8 us (5%)
  between operations  15.8 us (2%)
  blocking collectives  14.8 us (1%)
    unnamed x3, waiting for transfers between devices  522 us
    all_to_all x1, waiting for transfers between devices, shards(): lax.all_to_all(to_slots(grad_query), 'dp', split_axis=0, concat_axis=0, t...  72.3 us
    all_to_all x1, waiting for transfers between devices, shards(): lax.all_to_all(query_send, 'dp', split_axis=0, concat_axis=0, tiled=True)  49.2 us
    unnamed x18, local copies, waits for them, and re-layouts  46 us
    all_to_all x1, waiting for transfers between devices, shards(): lax.all_to_all(grad_send, 'dp', split_axis=0, concat_axis=0, tiled=True)  44.4 us
    all_gather x1, waiting for transfers between devices, project(): full_weight = lax.all_gather(w_value, 'fsdp', axis=0, tiled=True)  21.3 us
  transfers between devices with their start and end apart: 10, of which 10 were waited for; matrix products, arithmetic and copies ran while one was open for 17% of the time, Pallas kernels for 0%

commit v1 on v0

v1 whole, which is shorter than its diff:
```python
import functools

import jax
import jax.numpy as jnp
from jax import lax
from jax.experimental import pallas as pl
from jax.experimental.pallas import tpu as pltpu
from jax.sharding import PartitionSpec as P

MESH = pl.DeviceIdType.MESH
F32 = jnp.float32
BF16 = jnp.bfloat16
HD = 128
ROWS = 128
RANKS = 16
SLOTS = 16
KVH = 8
GROUP = 8
KVW = KVH * HD
HALF = 512
INV_ROOT = 1.0 / HD**0.5
LOG2E = 1.4426950408889634
CHIP_STEPS = ((1, 0), (3, 0), (0, 1), (1, 1), (3, 1), (2, 0), (2, 1))
LINE_STEPS = ((1, 0), (3, 0), (1, 1), (3, 1), (2, 0), (2, 1), (0, 1))


def dot(a, b):
    return jnp.dot(a, b, preferred_element_type=F32)


def dot_nt(a, b):
    return lax.dot_general(a, b, (((1,), (1,)), ((), ())), preferred_element_type=F32)


def dot_tn(a, b):
    return lax.dot_general(a, b, (((0,), (0,)), ((), ())), preferred_element_type=F32)


def device(y, zl, c, zh, x):
    return (y * 4 + zl * 2 + c, zh * 4 + x)


def kernel(
    li_ref, q_ref, k_ref, go_ref, w_ref, dest_ref, seg_ref,
    gq_ref, gk_ref, gi_ref, gw_ref,
    ka, va, qs, gos, xs, probs, li, wm, vp, vsib, vrow, dbuf, sb1, rb1, sb2, rb2, gva, gwb, gwr,
    sel, put, posl, startl, tmp,
    loc_sem, k_sem, kf_sem, v_sem, vf_sem, li_sem, w_sem, vs_sem, vx_sem,
    s1_sem, r1_sem, s2_sem, r2_sem, gx_sem, gf_sem, gi_sem, gws_sem, gwr_sem, out_sem,
):
    d, f = lax.axis_index("dp"), lax.axis_index("fsdp")
    y, zl, c = d // 4, lax.rem(d // 2, 2), lax.rem(d, 2)
    zh, x = f // 4, lax.rem(f, 4)
    z = zh * 2 + zl
    sib = device(y, zl, 1 - c, zh, x)

    def chip_at(step, sign):
        return lax.rem(y + sign * step[0] + 4, 4), lax.rem(zl + step[1], 2)

    def chip_dev(step, sign=1):
        ty, tz = chip_at(step, sign)
        return device(ty, tz, c, zh, x)

    def chip_index(step, sign=1):
        ty, tz = chip_at(step, sign)
        return ty * 2 + tz

    def line_at(step, sign=1):
        return lax.rem(x + sign * step[0] + 4, 4), lax.rem(c + step[1], 2)

    def line_dev(step, sign=1):
        tx, tc = line_at(step, sign)
        return device(y, zl, tc, zh, tx)

    def remote(src, dst, ssem, rsem, dev):
        return pltpu.make_async_remote_copy(
            src_ref=src, dst_ref=dst, send_sem=ssem, recv_sem=rsem, device_id=dev, device_id_type=MESH
        )

    own_k = pltpu.make_async_copy(k_ref, ka.at[d, pl.ds(0, ROWS)], loc_sem.at[0])
    own_k.start()
    q_loads = []
    for g in range(KVH):
        cols = pl.ds(g * 1024, 1024)
        a = pltpu.make_async_copy(q_ref.at[:, cols], dbuf.at[0, g], loc_sem.at[1 + g])
        b = pltpu.make_async_copy(go_ref.at[:, cols], dbuf.at[1, g], loc_sem.at[9 + g])
        a.start()
        b.start()
        q_loads += [(a, b)]
    me_line = c * 4 + x
    li_own = []
    for h in range(2):
        e = pltpu.make_async_copy(
            li_ref.at[:, pl.ds(pl.multiple_of(h * 4096 + x * 1024 + c * HALF, HALF), HALF)],
            li.at[h, me_line],
            loc_sem.at[17 + h],
        )
        e.start()
        li_own += [e]
    own_rows = w_ref.at[pl.ds(pl.multiple_of(c * HALF, HALF), HALF)]
    w_own = pltpu.make_async_copy(own_rows, wm.at[zh], loc_sem.at[19])
    w_own.start()

    barrier = pltpu.get_barrier_semaphore()

    def greet(dev):
        pl.semaphore_signal(barrier, inc=1, device_id=dev, device_id_type=MESH)

    w_dev = device(y, 1 - zl, c, 1 - zh, x)
    x_src = lax.rem(y, 2) * 2 + zl
    in_own_line = x == x_src
    for step in CHIP_STEPS:
        greet(chip_dev(step, -1))
    for step in LINE_STEPS:
        greet(line_dev(step, -1))
    greet(w_dev)
    for i in range(16):
        sy, sz = i // 4, i % 4

        @pl.when(jnp.logical_not(in_own_line & (y == sy) & (z == sz)))
        def _():
            greet(device(sy, sz % 2, c, sz // 2, x_src))

    pl.semaphore_wait(barrier, 7 + 7 + 1 + 16 - in_own_line.astype(jnp.int32))

    dest = jnp.broadcast_to(dest_ref[...], (SLOTS, ROWS))
    block = (dest >> 7).astype(F32)
    label = (dest & 127).astype(F32) + 1.0
    seg = jnp.broadcast_to(seg_ref[...], (SLOTS, ROWS)).astype(F32)
    ka[d, ROWS:, :] = jnp.concatenate(
        [block, label, seg] + [jnp.zeros((SLOTS, ROWS), F32)] * 5, axis=1
    ).astype(BF16)
    own_k.wait()

    def gather_start(buf, sems, fsems):
        copies = []
        for o, step in enumerate(CHIP_STEPS):
            r = remote(buf.at[d], buf.at[d], sems.at[0, o], sems.at[1, o], chip_dev(step))
            r.start()
            copies += [r]
        fwd = [remote(buf.at[d], buf.at[d], fsems.at[0, 7], fsems.at[1, 7], sib)]
        fwd[0].start()
        return copies, fwd

    k_copies, k_fwd = gather_start(ka, k_sem, kf_sem)
    li_copies = []
    for o, step in enumerate(LINE_STEPS):
        tx, tc = line_at(step)
        for h in range(2):
            r = remote(
                li_ref.at[:, pl.ds(pl.multiple_of(h * 4096 + tx * 1024 + tc * HALF, HALF), HALF)],
                li.at[h, me_line],
                li_sem.at[0, o * 2 + h],
                li_sem.at[1, o * 2 + h],
                line_dev(step),
            )
            r.start()
            li_copies += [r]
    w_copy = remote(own_rows, wm.at[zh], w_sem.at[0], w_sem.at[1], w_dev)
    w_copy.start()

    rows16 = lax.broadcasted_iota(jnp.int32, (SLOTS, ROWS), 0).astype(F32)
    tri = (
        lax.broadcasted_iota(jnp.int32, (ROWS, ROWS), 0)
        < lax.broadcasted_iota(jnp.int32, (ROWS, ROWS), 1)
    ).astype(F32).astype(BF16)
    ones = jnp.ones((ROWS, ROWS), BF16)
    rows256 = lax.broadcasted_iota(jnp.int32, (256, ROWS), 0).astype(F32)
    lane1 = lax.broadcasted_iota(jnp.int32, (ROWS, ROWS), 1).astype(F32) + 1.0
    lane1_256 = lax.broadcasted_iota(jnp.int32, (256, ROWS), 1).astype(F32) + 1.0
    low4 = (lax.broadcasted_iota(jnp.int32, (ROWS, ROWS), 0) & 15).astype(F32)

    def slots_of(block16):
        hot = (block16 == rows16).astype(F32)
        rank = jnp.sum(hot * dot(hot.astype(BF16), tri), axis=0, keepdims=True)
        return block16[0:1] * SLOTS + rank

    own_slot = slots_of(block)
    own_sel = (rows256 == own_slot).astype(F32).astype(BF16)

    for g in range(KVH):
        for which, dst in ((0, qs), (1, gos)):
            q_loads[g][which].wait()
            placed = dot(own_sel, dbuf[which, g]).astype(BF16)
            for h in range(GROUP):
                dst[:, g, h * SLOTS : (h + 1) * SLOTS, :] = placed[:, h * HD : (h + 1) * HD].reshape(
                    RANKS, SLOTS, HD
                )

    def take_keys(s):
        extra = ka[s, ROWS:, 0:384].astype(F32)
        block_s, label_s, seg_s = extra[:, 0:128], extra[:, 128:256], extra[:, 256:384]
        hot = (rows256 == slots_of(block_s)).astype(F32)
        hot_low = hot.astype(BF16)
        sel[s] = hot_low
        labels = dot((hot * label_s[0:1]).astype(BF16), ones)
        put[:, s] = (labels == lane1_256).astype(F32).astype(BF16).reshape(RANKS, SLOTS, ROWS)
        xs[:, s] = dot(hot_low, ka[s, 0:ROWS, :]).astype(BF16).reshape(RANKS, SLOTS, KVW)
        mine = (low4 + (s * SLOTS).astype(F32) == own_slot).astype(F32)
        columns = dot((mine * label[0:1]).astype(BF16), ones)
        at_row = (columns == lane1).astype(F32).astype(BF16)
        posl[s] = dot_nt(label.astype(BF16), mine.astype(BF16)) - 1.0
        startl[s] = dot_nt(seg_s.astype(BF16), at_row)

    def take_values(s):
        xs[:, s] = dot(sel[s], va[s]).astype(BF16).reshape(RANKS, SLOTS, KVW)

    def gather_finish(buf, sems, fsems, copies, fwd, take):
        take(d)
        fwd[0].wait_recv()
        take(y * 4 + zl * 2 + 1 - c)
        pending = None
        for o, step in enumerate(CHIP_STEPS):
            src = chip_index(step, -1) * 2 + c
            copies[o].wait_recv()
            r = remote(buf.at[src], buf.at[src], fsems.at[0, o], fsems.at[1, o], sib)
            r.start()
            fwd += [r]
            take(src)
            if pending is not None:
                pending[0].wait_recv()
                take(pending[1])
            pending = (r, chip_index(step, -1) * 2 + 1 - c)
        pending[0].wait_recv()
        take(pending[1])

    gather_finish(ka, k_sem, kf_sem, k_copies, k_fwd, take_keys)

    for e in li_own:
        e.wait()
    w_own.wait()
    for r in li_copies:
        r.wait_recv()
    w_copy.wait_recv()

    def value_term(core):
        def chunk(n, _):
            cols = pl.ds(pl.multiple_of(n * 256, 256), 256)
            part = dot(li[0, pl.ds(core * 4, 4)].reshape(HALF, HALF), wm[0, :, cols])
            part += dot(li[1, pl.ds(core * 4, 4)].reshape(HALF, HALF), wm[1, :, cols])
            vp[pl.ds(core * 4, 4), :, cols] = part.astype(BF16).reshape(4, ROWS, 256)
            return 0

        lax.fori_loop(0, 4, chunk, 0)

    value_term(1 - c)
    v_sib = remote(
        vp.at[pl.ds((1 - c) * 4, 4)], vsib, vs_sem.at[0], vs_sem.at[1], sib
    )
    v_sib.start()
    value_term(c)

    for r in k_copies + k_fwd:
        r.wait_send()

    def mask_of(t):
        j = lax.broadcasted_iota(jnp.int32, (ROWS, ROWS), 0).astype(F32)
        return (j <= posl[t][0:1]) & (j >= startl[t][0:1])

    def first_pass(t, _):
        put_t = put[t].reshape(256, ROWS)
        ka[t, 0:ROWS, :] = dot_tn(put_t, xs[t].reshape(256, KVW)).astype(BF16)
        allowed = mask_of(t)
        for g in range(KVH):
            cols = slice(g * HD, (g + 1) * HD)
            scores = dot_nt(ka[t, 0:ROWS, cols], qs[t, g]) * (INV_ROOT * LOG2E)
            scores = jnp.where(allowed, scores, -1e30)
            peak = jnp.maximum(jnp.max(scores, axis=0, keepdims=True), -1e29)
            expo = jnp.exp2(scores - peak)
            total = jnp.maximum(jnp.sum(expo, axis=0, keepdims=True), 0.5)
            low = (expo * (1.0 / total)).astype(BF16)
            probs[t, g] = low
            tmp[:, cols] = dot(low, gos[t, g]).astype(BF16)
        xs[t] = dot(put_t, tmp[...]).astype(BF16).reshape(RANKS, SLOTS, KVW)
        return 0

    lax.fori_loop(0, 8, first_pass, 0)

    v_sib.wait_recv()
    vx = []
    own_v = None
    for o, dx in enumerate((0, 1, 3, 2)):
        tx = lax.rem(x + dx, 4)
        total = vp[c * 4 + tx].astype(F32) + vsib[tx].astype(F32)
        if dx == 0:
            own_v = total
        else:
            vp[c * 4 + tx] = total.astype(BF16)
            r = remote(
                vp.at[c * 4 + tx], vrow.at[o - 1], vx_sem.at[0, o - 1], vx_sem.at[1, o - 1],
                device(y, zl, c, zh, tx),
            )
            r.start()
            vx += [r]

    lax.fori_loop(8, 16, first_pass, 0)

    vsum = own_v
    for o in range(3):
        vx[o].wait_recv()
        vsum = vsum + vrow[o].astype(F32)
    va[d] = vsum.astype(BF16)
    v_copies, v_fwd = gather_start(va, v_sem, vf_sem)

    def scatter_start(sb, rb, ssems, rsems):
        sib_copies, out_copies = [], []
        for q in range(8):
            s = q * 2 + 1 - c
            dbuf[1 - c, q] = dot_tn(sel[s], xs[:, s].reshape(256, KVW)).astype(BF16)
            r = remote(dbuf.at[1 - c, q], sb.at[q], ssems.at[0, q], ssems.at[1, q], sib)
            r.start()
            sib_copies += [r]
        for r in sib_copies:
            r.wait_recv()
        for o, step in enumerate(CHIP_STEPS + ((0, 0),)):
            q = chip_index(step)
            s = q * 2 + c
            part = dot_tn(sel[s], xs[:, s].reshape(256, KVW)) + sb[q].astype(F32)
            dbuf[c, q] = part.astype(BF16)
            if o < 7:
                r = remote(dbuf.at[c, q], rb.at[o], rsems.at[0, o], rsems.at[1, o], chip_dev(step))
                r.start()
                out_copies += [r]
        return sib_copies, out_copies

    def scatter_finish(rb, out_copies):
        total = dbuf[c, y * 2 + zl].astype(F32)
        for o in range(7):
            out_copies[o].wait_recv()
            total = total + rb[o].astype(F32)
        return total.astype(BF16)

    s1_copies, r1_copies = scatter_start(sb1, rb1, s1_sem, r1_sem)
    gva[me_line] = scatter_finish(rb1, r1_copies)

    gx = []
    gf = []
    for o, dx in enumerate((1, 3, 2)):
        r = remote(
            gva.at[me_line], gva.at[me_line], gx_sem.at[0, o], gx_sem.at[1, o],
            device(y, zl, c, zh, lax.rem(x + dx, 4)),
        )
        r.start()
        gx += [r]
    r = remote(gva.at[me_line], gva.at[me_line], gf_sem.at[0, 3], gf_sem.at[1, 3], sib)
    r.start()
    gf += [r]
    for o, dx in enumerate((1, 3, 2)):
        src = c * 4 + lax.rem(x - dx + 4, 4)
        gx[o].wait_recv()
        r = remote(gva.at[src], gva.at[src], gf_sem.at[0, o], gf_sem.at[1, o], sib)
        r.start()
        gf += [r]
    for r in vx + [v_sib]:
        r.wait_send()
    for r in gf:
        r.wait_recv()

    def input_term(j, _):
        for h in range(2):
            vp[j, :, h * HALF : (h + 1) * HALF] = dot_nt(gva[j], wm[h]).astype(BF16)
        return 0

    lax.fori_loop(0, 8, input_term, 0)
    gi_cols = [pl.ds(pl.multiple_of(h * 4096 + x * 1024 + c * HALF, HALF), HALF) for h in range(2)]
    gi_copies = []
    gi_own = []
    for h in range(2):
        e = pltpu.make_async_copy(
            vp.at[me_line, :, pl.ds(h * HALF, HALF)], gi_ref.at[:, gi_cols[h]], loc_sem.at[20 + h]
        )
        e.start()
        gi_own += [e]
    for o, step in enumerate(LINE_STEPS):
        tx, tc = line_at(step)
        for h in range(2):
            r = remote(
                vp.at[tc * 4 + tx, :, pl.ds(h * HALF, HALF)], gi_ref.at[:, gi_cols[h]],
                gi_sem.at[0, o * 2 + h], gi_sem.at[1, o * 2 + h], line_dev(step),
            )
            r.start()
            gi_copies += [r]

    def weight_term(n, _):
        h, cols = n // 4, pl.ds(pl.multiple_of(lax.rem(n, 4) * 256, 256), 256)
        part = dot_tn(li[h].reshape(1024, HALF), gva[:, :, cols].reshape(1024, 256))
        gwb[h, :, :, cols] = part.astype(BF16).reshape(8, 64, 256)
        return 0

    lax.fori_loop(0, 8, weight_term, 0)
    my_slot = y * 4 + z
    for h in range(2):
        for fb in range(8):
            to_self = in_own_line & (y // 2 == h) & (f == fb)
            dev = device(2 * h + x // 2, lax.rem(x, 2), c, fb // 4, fb % 4)

            @pl.when(to_self)
            def _():
                pltpu.make_async_copy(gwb.at[h, fb], gwr.at[my_slot], gwr_sem.at[my_slot]).start()

            @pl.when(jnp.logical_not(to_self))
            def _():
                remote(
                    gwb.at[h, fb], gwr.at[my_slot], gws_sem.at[h * 8 + fb], gwr_sem.at[my_slot], dev
                ).start()

    gather_finish(va, v_sem, vf_sem, v_copies, v_fwd, take_values)

    def second_pass(t, _):
        put_t = put[t].reshape(256, ROWS)
        tmp[...] = dot_tn(put_t, xs[t].reshape(256, KVW)).astype(BF16)
        for g in range(KVH):
            cols = slice(g * HD, (g + 1) * HD)
            grad = gos[t, g]
            grad_probs = dot_nt(tmp[:, cols], grad)
            low = probs[t, g].astype(F32)
            row_dots = jnp.sum(low * grad_probs, axis=0, keepdims=True)
            grad_scores = (low * (grad_probs - row_dots)).astype(BF16)
            tmp[:, cols] = (dot(grad_scores, qs[t, g]) * INV_ROOT).astype(BF16)
            qs[t, g] = (dot_tn(grad_scores, ka[t, 0:ROWS, cols]) * INV_ROOT).astype(BF16)
        xs[t] = dot(put_t, tmp[...]).astype(BF16).reshape(RANKS, SLOTS, KVW)
        return 0

    lax.fori_loop(0, 16, second_pass, 0)
    for r in s1_copies + r1_copies + v_copies + v_fwd:
        r.wait_send()
    s2_copies, r2_copies = scatter_start(sb2, rb2, s2_sem, r2_sem)

    q_out = []
    for g in range(KVH):
        slots = jnp.concatenate(
            [qs[:, g, h * SLOTS : (h + 1) * SLOTS, :].reshape(256, HD) for h in range(GROUP)], axis=1
        )
        va[g] = dot_tn(own_sel, slots).astype(BF16)
        e = pltpu.make_async_copy(va.at[g], gq_ref.at[:, pl.ds(g * 1024, 1024)], out_sem.at[g])
        e.start()
        q_out += [e]

    gw_total = jnp.zeros((64, KVW), F32)
    for i in range(16):
        pltpu.make_async_copy(gwr.at[i], gwr.at[i], gwr_sem.at[i]).wait()
        gw_total = gw_total + gwr[i].astype(F32)
    gw_ref[...] = gw_total
    gk_ref[...] = scatter_finish(rb2, r2_copies)

    for r in gi_copies:
        r.wait()
    for e in gi_own + q_out:
        e.wait()
    for r in li_copies + [w_copy] + s2_copies + r2_copies + gx + gf:
        r.wait_send()
    for h in range(2):
        for fb in range(8):
            to_self = in_own_line & (y // 2 == h) & (f == fb)

            @pl.when(jnp.logical_not(to_self))
            def _():
                remote(
                    gwb.at[h, fb], gwr.at[my_slot], gws_sem.at[h * 8 + fb], gwr_sem.at[my_slot],
                    device(2 * h + x // 2, lax.rem(x, 2), c, fb // 4, fb % 4),
                ).wait_send()


def shards(layer_input, queries, key_rows, grad_out, w_value, destination, seg_start):
    any_spec = pl.BlockSpec(memory_space=pl.ANY)
    vmem_spec = pl.BlockSpec(memory_space=pltpu.VMEM)
    dma = pltpu.SemaphoreType.DMA
    tokens = pltpu.VMEM
    return pl.pallas_call(
        kernel,
        out_shape=(
            jax.ShapeDtypeStruct(queries.shape, BF16),
            jax.ShapeDtypeStruct(key_rows.shape, BF16),
            jax.ShapeDtypeStruct(layer_input.shape, BF16),
            jax.ShapeDtypeStruct((64, KVW), F32),
        ),
        in_specs=[any_spec] * 5 + [vmem_spec] * 2,
        out_specs=(any_spec, vmem_spec, any_spec, vmem_spec),
        scratch_shapes=[
            tokens((RANKS, ROWS + SLOTS, KVW), BF16),
            tokens((RANKS, ROWS, KVW), BF16),
            tokens((RANKS, KVH, ROWS, HD), BF16),
            tokens((RANKS, KVH, ROWS, HD), BF16),
            tokens((RANKS, RANKS, SLOTS, KVW), BF16),
            tokens((RANKS, KVH, ROWS, ROWS), BF16),
            tokens((2, 8, ROWS, HALF), BF16),
            tokens((2, HALF, KVW), BF16),
            tokens((8, ROWS, KVW), BF16),
            tokens((4, ROWS, KVW), BF16),
            tokens((3, ROWS, KVW), BF16),
            tokens((2, 8, ROWS, KVW), BF16),
            tokens((8, ROWS, KVW), BF16),
            tokens((7, ROWS, KVW), BF16),
            tokens((8, ROWS, KVW), BF16),
            tokens((7, ROWS, KVW), BF16),
            tokens((8, ROWS, KVW), BF16),
            tokens((2, 8, 64, KVW), BF16),
            tokens((16, 64, KVW), BF16),
            tokens((RANKS, 256, ROWS), BF16),
            tokens((RANKS, RANKS, SLOTS, ROWS), BF16),
            tokens((RANKS, SLOTS, ROWS), F32),
            tokens((RANKS, SLOTS, ROWS), F32),
            tokens((ROWS, KVW), BF16),
            dma((22,)),
            dma((2, 7)),
            dma((2, 8)),
            dma((2, 7)),
            dma((2, 8)),
            dma((2, 14)),
            dma((2,)),
            dma((2,)),
            dma((2, 3)),
            dma((2, 8)),
            dma((2, 7)),
            dma((2, 8)),
            dma((2, 7)),
            dma((2, 3)),
            dma((2, 4)),
            dma((2, 14)),
            dma((16,)),
            dma((16,)),
            dma((8,)),
        ],
        name="packed_backward",
        compiler_params=pltpu.CompilerParams(
            collective_id=0, has_side_effects=True, vmem_limit_bytes=64 * 1024 * 1024
        ),
    )(
        layer_input, queries, key_rows, grad_out, w_value,
        destination.reshape(1, ROWS), seg_start.reshape(1, ROWS),
    )


def solution(mesh):
    both = P(("dp", "fsdp"), None)
    return jax.shard_map(
        shards,
        mesh=mesh,
        in_specs=(both, both, both, both, P("fsdp", None), P(("dp", "fsdp")), P(("dp", "fsdp"))),
        out_specs=(both, both, both, both),
        check_vma=False,
    )
```

time: 999 us -> 253 us (0.25); the launches traced: 983 us -> 251 us
  waiting for transfers between devices: 729 us -> 0 us
  Pallas kernels: 0 us -> 244 us
  local copies, waits for them, and re-layouts: 88.9 us -> 5.98 us
  matrix products: 74.7 us -> 0 us
  starting transfers between devices: 51.8 us -> 0 us
  between operations: 15.8 us -> 0.66 us
  blocking collectives: 14.8 us -> 0 us
    unnamed x3 -> x0, waiting for transfers between devices: 522 us -> none
    pallas_call x0 -> x1, Pallas kernels: none -> 244 us  [shards(): pl.pallas_call(kernel, out_shape=(jax.ShapeDtypeStruct(queries.shape, BF1...]
    all_to_all x8 -> x0, waiting for transfers between devices: 185 us -> none  [the longest x1 72.3 us: shards(): lax.all_to_all(to_slots(grad_query), 'dp', split_axis=0, concat_axis=0, t...]
    dot_general x23 -> x0, matrix products: 74.7 us -> none  [the longest x4 17.4 us: gather_slots(): jnp.dot(picker, data, preferred_element_type=jnp.float32)]
    all_to_all x8 -> x0, starting transfers between devices: 51.5 us -> none  [the longest x1 11.1 us: shards(): lax.all_to_all(query_send, 'dp', split_axis=0, concat_axis=0, tiled=True)]
    unnamed x18 -> x10, local copies, waits for them, and re-layouts: 46 us -> 5.98 us
    reshape x16 -> x0, local copies, waits for them, and re-layouts: 33.3 us -> none  [the longest x4 11.3 us: gather_slots(): return jnp.dot(picker, data, preferred_element_type=jnp.float32).astype(j...]
    all_gather x1 -> x0, waiting for transfers between devices: 21.3 us -> none  [project(): full_weight = lax.all_gather(w_value, 'fsdp', axis=0, tiled=True)]
  transfers between devices with their start and end apart: 10 -> 0, of which waited for: 10 -> 0; matrix products, arithmetic and copies ran while one was open for 17% -> 0% of each run, Pallas kernels for 0% -> 0%
where the time goes in v1:
time: 253 us; the launch traced here: 251 us
  Pallas kernels  244 us (96%)
  local copies, waits for them, and re-layouts  5.98 us (2%)
    pallas_call x1, Pallas kernels, shards(): pl.pallas_call(kernel, out_shape=(jax.ShapeDtypeStruct(queries.shape, BF1...  244 us
    unnamed x10, local copies, waits for them, and re-layouts  5.98 us

profile of v1, /device:TPU:1, one launch (start us, length us, event | category | flops | bytes accessed | tf_op | source)
XLA Modules:
  0.0 251.1 jit_solution(10682711613424336995)
XLA Ops:
  0.6 244.4 %packed_backward.1 = (bf16[128,8192]{1,0:T(8,128)(2,1)}, bf16[128,1024]{1,0:T(8,128)(2,1)}, bf16[128,8192]{1,0:T(8,128)(2,1)}, f32[64,1024]{1,0:T(8,128)}) custom-call(bf16[128,8192]{1,0:T(8,128)(2,1)} %li_ref.1, bf16[128,8192]{1,0:T(8,128)(2,1)} %q_ref.1, bf16[128,1024]{1,0:T(8,128)(2,1)} %k_ref.1, bf16[128,8192]{1,0:T(8,128)(2,1)} %go_ref.1, ...), custom_call_target="tpu_custom_call" | custom-call | tf_op jit(solution)/shard_map/packed_backward/pallas_call | solution.py:469
  245.1 0.0 copy-start.2
  245.1 0.0 copy-start
  245.1 3.2 %copy.15 = bf16[128,8192]{1,0:T(8,128)(2,1)} copy(bf16[128,8192]{1,0:T(8,128)(2,1)} %get-tuple-element.8) | data formatting | bytes 4194304
  248.3 0.0 copy-done.2
  248.3 0.7 copy.16
  249.0 0.0 copy-done
  249.0 0.0 copy-start.1
  249.0 1.3 copy.17
  250.4 0.0 copy-done.1
  250.4 0.7 copy.18
Async XLA Ops:
  245.1 3.3 %copy-start.2 = (bf16[128,1024]{1,0:T(8,128)(2,1)S(1)}, bf16[128,1024]{1,0:T(8,128)(2,1)}, u32[]{:S(2)}) copy-start(bf16[128,1024]{1,0:T(8,128)(2,1)} %get-tuple-element.9) | copy-start | bytes 786436
  245.1 4.0 %copy-start = (bf16[128,8192]{1,0:T(8,128)(2,1)S(1)}, bf16[128,8192]{1,0:T(8,128)(2,1)}, u32[]{:S(2)}) copy-start(bf16[128,8192]{1,0:T(8,128)(2,1)} %get-tuple-element.10) | copy-start | bytes 6291460
  249.0 1.3 copy-start.1

commit v2 on v1

v2 whole, which is shorter than its diff:
```python
import functools

import jax
import jax.numpy as jnp
from jax import lax
from jax.experimental import pallas as pl
from jax.experimental.pallas import tpu as pltpu
from jax.sharding import PartitionSpec as P

MESH = pl.DeviceIdType.MESH
F32 = jnp.float32
BF16 = jnp.bfloat16
HD = 128
ROWS = 128
RANKS = 16
SLOTS = 16
KVH = 8
GROUP = 8
KVW = KVH * HD
HALF = 512
KEYS = 160
INV_ROOT = 1.0 / HD**0.5
LOG2E = 1.4426950408889634
LINE_STEPS = ((1, 0), (3, 0), (1, 1), (3, 1), (2, 0), (2, 1), (0, 1))


def dot(a, b):
    return jnp.dot(a, b, preferred_element_type=F32)


def dot_nt(a, b):
    return lax.dot_general(a, b, (((1,), (1,)), ((), ())), preferred_element_type=F32)


def dot_tn(a, b):
    return lax.dot_general(a, b, (((0,), (0,)), ((), ())), preferred_element_type=F32)


def device(y, zl, c, zh, x):
    return (y * 4 + zl * 2 + c, zh * 4 + x)


def kernel(
    li_ref, q_ref, k_ref, go_ref, w_ref, dest_ref, seg_ref,
    gq_ref, gk_ref, gi_ref, gw_ref,
    ka, va, qs, gos, xa, xb, probs, li, wm, vp, vsib, vrow, sb1, rb1, sb2, rb2, gva,
    ga, gb, ra, rbb, gwa, gwb, sel, selo, labk, labo, posl, startl,
    loc_sem, k_sem, kf_sem, v_sem, vf_sem, li_sem, w_sem, vs_sem, vx_sem,
    s1_sem, r1_sem, s2_sem, r2_sem, gx_sem, gf_sem, gi_sem, g1_sem, g2s_sem, g2r_sem, out_sem,
):
    d, f = lax.axis_index("dp"), lax.axis_index("fsdp")
    y, zl, c = d // 4, lax.rem(d // 2, 2), lax.rem(d, 2)
    zh, x = f // 4, lax.rem(f, 4)
    z = zh * 2 + zl
    sib = device(y, zl, 1 - c, zh, x)
    y_up, y_down, y_far = lax.rem(y + 1, 4), lax.rem(y + 3, 4), lax.rem(y + 2, 4)
    dev_up, dev_down = device(y_up, zl, c, zh, x), device(y_down, zl, c, zh, x)
    dev_z = device(y, 1 - zl, c, zh, x)

    def line_at(step, sign=1):
        return lax.rem(x + sign * step[0] + 4, 4), lax.rem(c + step[1], 2)

    def line_dev(step, sign=1):
        tx, tc = line_at(step, sign)
        return device(y, zl, tc, zh, tx)

    def remote(src, dst, ssem, rsem, dev):
        return pltpu.make_async_remote_copy(
            src_ref=src, dst_ref=dst, send_sem=ssem, recv_sem=rsem, device_id=dev, device_id_type=MESH
        )

    own_k = pltpu.make_async_copy(k_ref, ka.at[d, pl.ds(0, ROWS)], loc_sem.at[0])
    own_k.start()

    def load(ref, g, sem):
        e = pltpu.make_async_copy(ref.at[:, pl.ds(g * 1024, 1024)], vp.at[g], sem)
        e.start()
        return e

    q_loads = [load(q_ref, g, loc_sem.at[1 + g]) for g in range(KVH)]
    me_line = c * 4 + x
    li_own = []
    for h in range(2):
        e = pltpu.make_async_copy(
            li_ref.at[:, pl.ds(pl.multiple_of(h * 4096 + x * 1024 + c * HALF, HALF), HALF)],
            li.at[h, me_line],
            loc_sem.at[17 + h],
        )
        e.start()
        li_own += [e]
    own_rows = w_ref.at[pl.ds(pl.multiple_of(c * HALF, HALF), HALF)]
    w_own = pltpu.make_async_copy(own_rows, wm.at[zh], loc_sem.at[19])
    w_own.start()

    barrier = pltpu.get_barrier_semaphore()

    def greet(dev):
        pl.semaphore_signal(barrier, inc=1, device_id=dev, device_id_type=MESH)

    w_dev = device(y, 1 - zl, c, 1 - zh, x)
    z_devs = [device(y, lax.rem(z + i, 2), c, lax.rem(z + i, 4) // 2, x) for i in (1, 2, 3)]
    y_devs = [device(lax.rem(y + i, 4), zl, c, zh, x) for i in (1, 2, 3)]
    x_src = lax.rem(y, 2) * 2 + zl
    in_own_line = x == x_src
    for dev in [dev_up, dev_down, dev_z, w_dev] + z_devs + y_devs:
        greet(dev)
    for step in LINE_STEPS:
        greet(line_dev(step, -1))
    y_src = 2 * (y // 2) + x // 2
    for i in range(4):

        @pl.when(jnp.logical_not(in_own_line & (y == i) & (zl == lax.rem(x, 2))))
        def _():
            greet(device(i, lax.rem(x, 2), c, zh, x_src))

        @pl.when(jnp.logical_not(in_own_line & (y == y_src) & (z == i)))
        def _():
            greet(device(y_src, i % 2, c, i // 2, x_src))

    pl.semaphore_wait(barrier, 10 + 7 + 8 - 2 * in_own_line.astype(jnp.int32))

    dest = jnp.broadcast_to(dest_ref[...], (SLOTS, ROWS))
    block = (dest >> 7).astype(F32)
    label = (dest & 127).astype(F32) + 1.0
    seg = jnp.broadcast_to(seg_ref[...], (SLOTS, ROWS)).astype(F32)
    ka[d, ROWS:, :] = jnp.concatenate(
        [block, label, seg] + [jnp.zeros((SLOTS, ROWS), F32)] * 5, axis=1
    ).astype(BF16)
    own_k.wait()

    class Gather:
        def __init__(self, buf, rows, sems, fsems):
            chips = [(y, zl), (y, 1 - zl), (y_down, zl), (y_up, zl)]
            chips += [(y_down, 1 - zl), (y_up, 1 - zl), (y_far, zl), (y_far, 1 - zl)]
            self.q = [cy * 2 + cz for cy, cz in chips]
            me, zs, yd, yu, _, _, yo, _ = [q * 2 + c for q in self.q]

            def hop(i, slot, dev, first=0, count=rows):
                part = buf.at[slot, pl.ds(first, count)]
                return remote(part, part, sems.at[0, i], sems.at[1, i], dev)

            self.hops = [
                hop(0, me, dev_up), hop(1, me, dev_down), hop(2, me, dev_z),
                hop(3, zs, dev_up), hop(4, zs, dev_down),
                hop(5, yd, dev_up, 0, 64), hop(6, yu, dev_down, 64, rows - 64),
                hop(7, yo, dev_z),
            ]
            self.twin = [
                remote(buf.at[q * 2 + c], buf.at[q * 2 + c], fsems.at[0, j], fsems.at[1, j], sib)
                for j, q in enumerate(self.q)
            ]

        def start(self):
            for r in self.hops[:3] + self.twin[:1]:
                r.start()

        def second(self):
            hops, twin = self.hops, self.twin
            hops[2].wait_recv()
            for r in (hops[3], hops[4], twin[1]):
                r.start()
            hops[0].wait_recv()
            for r in (hops[5], twin[2]):
                r.start()
            hops[1].wait_recv()
            for r in (hops[6], twin[3]):
                r.start()

        def third(self):
            hops, twin = self.hops, self.twin
            hops[5].wait_recv()
            hops[6].wait_recv()
            for r in (hops[7], twin[6]):
                r.start()
            hops[3].wait_recv()
            twin[4].start()
            hops[4].wait_recv()
            twin[5].start()

        def fourth(self):
            self.hops[7].wait_recv()
            self.twin[7].start()

        def take(self, which, taker):
            for j in which:
                self.twin[j].wait_recv()
                taker(self.q[j])

        def drain(self):
            for r in self.hops + self.twin:
                r.wait_send()

    keys = Gather(ka, ROWS + SLOTS, k_sem, kf_sem)
    keys.start()
    li_copies = []
    for o, step in enumerate(LINE_STEPS):
        tx, tc = line_at(step)
        for h in range(2):
            r = remote(
                li_ref.at[:, pl.ds(pl.multiple_of(h * 4096 + tx * 1024 + tc * HALF, HALF), HALF)],
                li.at[h, me_line],
                li_sem.at[0, o * 2 + h],
                li_sem.at[1, o * 2 + h],
                line_dev(step),
            )
            r.start()
            li_copies += [r]
    w_copy = remote(own_rows, wm.at[zh], w_sem.at[0], w_sem.at[1], w_dev)
    w_copy.start()

    rows16 = lax.broadcasted_iota(jnp.int32, (SLOTS, ROWS), 0).astype(F32)
    tri = (
        lax.broadcasted_iota(jnp.int32, (ROWS, ROWS), 0)
        < lax.broadcasted_iota(jnp.int32, (ROWS, ROWS), 1)
    ).astype(F32).astype(BF16)
    ones = jnp.ones((ROWS, ROWS), BF16)
    rows256 = lax.broadcasted_iota(jnp.int32, (256, ROWS), 0).astype(F32)
    lane1 = lax.broadcasted_iota(jnp.int32, (ROWS, ROWS), 1).astype(F32) + 1.0
    low4 = (lax.broadcasted_iota(jnp.int32, (ROWS, ROWS), 0) & 15).astype(F32)

    def ranks_of(block16):
        hot = (block16 == rows16).astype(F32)
        return jnp.sum(hot * dot(hot.astype(BF16), tri), axis=0, keepdims=True)

    own_slot = block[0:1] * SLOTS + ranks_of(block)
    own_sel = (rows256 == own_slot).astype(F32).astype(BF16)

    def by_block(g, dst):
        placed = dot(own_sel, vp[g]).astype(BF16)
        for h in range(GROUP):
            dst[:, g, h * SLOTS : (h + 1) * SLOTS, :] = placed[:, h * HD : (h + 1) * HD].reshape(
                RANKS, SLOTS, HD
            )

    go_loads = []
    for g in range(KVH):
        q_loads[g].wait()
        by_block(g, qs)
        go_loads += [load(go_ref, g, loc_sem.at[9 + g])]
    keys.second()
    for g in range(KVH):
        go_loads[g].wait()
        by_block(g, gos)

    def take_keys(q):
        for core in range(2):
            s = q * 2 + core
            extra = ka[s, ROWS:, 0:384].astype(F32)
            block_s, label_s, seg_s = extra[:, 0:128], extra[:, 128:256], extra[:, 256:384]
            rank = ranks_of(block_s)
            base = block_s[0:1] * SLOTS
            main = jnp.where(rank < 8.0, base + core * 8 + rank, -1.0)
            slot8 = (lax.rem(s, 8) * 2).astype(F32)
            over = jnp.where(rank < 8.0, -1.0, base + slot8 + rank - 8.0)
            hot = (rows256 == main).astype(F32)
            sel[q, :, core * ROWS : (core + 1) * ROWS] = hot.astype(BF16)
            hot_over = (rows256 == over).astype(F32)
            lanes = pl.ds(pl.multiple_of(lax.rem(s, 8) * ROWS, ROWS), ROWS)
            selo[s // 8, :, lanes] = hot_over.astype(BF16)
            marks = dot((hot * label_s[0:1]).astype(BF16), ones)
            marks = marks if core == 0 else marks + before
            before = marks
            labo[s // 8] += dot((hot_over * label_s[0:1]).astype(BF16), ones)
            mine = (low4 + (s * SLOTS).astype(F32) == own_slot).astype(F32)
            columns = dot((mine * label[0:1]).astype(BF16), ones)
            at_row = (columns == lane1).astype(F32).astype(BF16)
            posl[s] = dot_nt(label.astype(BF16), mine.astype(BF16))
            startl[s] = dot_nt(seg_s.astype(BF16), at_row) + 1.0
        labk[:, q] = marks.astype(BF16).reshape(RANKS, SLOTS, ROWS)
        take_pair(ka, xa, q)

    def take_pair(buf, dst, q):
        pair = buf[pl.ds(q * 2, 2), 0:ROWS, :].reshape(2 * ROWS, KVW)
        dst[:, q] = dot(sel[q], pair).astype(BF16).reshape(RANKS, SLOTS, KVW)

    def take_over(buf, dst):
        for half in range(2):
            rows = buf[half * 8 : half * 8 + 8, 0:ROWS, :].reshape(8 * ROWS, KVW)
            dst[:, 8 + half] = dot(selo[half], rows).astype(BF16).reshape(RANKS, SLOTS, KVW)

    labo[...] = jnp.zeros_like(labo)
    keys.take((0,), take_keys)
    keys.third()
    keys.take((1, 2, 3), take_keys)
    keys.fourth()
    keys.take((4, 5, 6, 7), take_keys)
    take_over(ka, xa)
    for half in range(2):
        labk[:, 8 + half] = labo[half].astype(BF16).reshape(RANKS, SLOTS, ROWS)

    def first_pass(t, _):
        marks = labk[t].reshape(KEYS, ROWS).astype(F32)
        bias = jnp.where((marks <= posl[t][0:1]) & (marks >= startl[t][0:1]), 0.0, -1e30)
        for g in range(KVH):
            cols = slice(g * HD, (g + 1) * HD)
            scores = dot_nt(xa[t, :, :, cols].reshape(KEYS, HD), qs[t, g]) * (INV_ROOT * LOG2E) + bias
            peak = jnp.maximum(jnp.max(scores, axis=0, keepdims=True), -1e29)
            expo = jnp.exp2(scores - peak)
            total = jnp.maximum(jnp.sum(expo, axis=0, keepdims=True), 0.5)
            low = (expo * (1.0 / total)).astype(BF16)
            probs[t, g] = low
            xb[t, :, :, cols] = dot(low, gos[t, g]).astype(BF16).reshape(10, SLOTS, HD)
        return 0

    lax.fori_loop(0, 4, first_pass, 0)

    for e in li_own:
        e.wait()
    w_own.wait()
    for r in li_copies:
        r.wait_recv()
    w_copy.wait_recv()

    def value_term(core):
        def chunk(n, _):
            cols = pl.ds(pl.multiple_of(n * 256, 256), 256)
            part = dot(li[0, pl.ds(core * 4, 4)].reshape(HALF, HALF), wm[0, :, cols])
            part += dot(li[1, pl.ds(core * 4, 4)].reshape(HALF, HALF), wm[1, :, cols])
            vp[pl.ds(core * 4, 4), :, cols] = part.astype(BF16).reshape(4, ROWS, 256)
            return 0

        lax.fori_loop(0, 4, chunk, 0)

    value_term(1 - c)
    v_sib = remote(vp.at[pl.ds((1 - c) * 4, 4)], vsib, vs_sem.at[0], vs_sem.at[1], sib)
    v_sib.start()
    value_term(c)
    lax.fori_loop(4, 6, first_pass, 0)

    v_sib.wait_recv()
    vx = []
    own_v = None
    for o, dx in enumerate((2, 1, 3)):
        tx = lax.rem(x + dx, 4)
        vp[c * 4 + tx] = (vp[c * 4 + tx].astype(F32) + vsib[tx].astype(F32)).astype(BF16)
        r = remote(
            vp.at[c * 4 + tx], vrow.at[o], vx_sem.at[0, o], vx_sem.at[1, o],
            device(y, zl, c, zh, tx),
        )
        r.start()
        vx += [r]
    lax.fori_loop(6, 16, first_pass, 0)
    keys.drain()

    class Scatter:
        def __init__(self, sb, rb, ssems, rsems):
            self.sb, self.rb = sb, rb
            self.twin = [
                remote(self.block(q, 1 - c), sb.at[q], ssems.at[0, q], ssems.at[1, q], sib)
                for q in range(8)
            ]
            oz = 1 - zl
            plan = (
                (y_far * 2 + oz, 0, 0, ROWS, dev_z), (y_up * 2 + oz, 1, 0, ROWS, dev_up),
                (y_down * 2 + oz, 2, 0, ROWS, dev_down),
                (y_far * 2 + zl, 3, 0, 64, dev_up), (y_far * 2 + zl, 3, 64, 64, dev_down),
                (y * 2 + oz, 4, 0, ROWS, dev_z),
                (y_up * 2 + zl, 5, 0, ROWS, dev_up), (y_down * 2 + zl, 6, 0, ROWS, dev_down),
            )
            self.hops = [
                remote(
                    ka.at[c * 8 + q, pl.ds(first, count)], rb.at[slot, pl.ds(first, count)],
                    rsems.at[0, i], rsems.at[1, i], dev,
                )
                for i, (q, slot, first, count, dev) in enumerate(plan)
            ]

        def block(self, q, core):
            return ka.at[core * 8 + q, pl.ds(0, ROWS)]

        def part(self, q, core):
            s = q * 2 + core
            lanes = pl.ds(pl.multiple_of(core * ROWS, ROWS), ROWS)
            total = dot_tn(sel[q, :, lanes], xb[:, q].reshape(256, KVW))
            lanes = pl.ds(pl.multiple_of(lax.rem(s, 8) * ROWS, ROWS), ROWS)
            return total + dot_tn(selo[s // 8, :, lanes], xb[:, 8 + s // 8].reshape(256, KVW))

        def start(self):
            for q in range(8):
                ka[(1 - c) * 8 + q, 0:ROWS, :] = self.part(q, 1 - c).astype(BF16)
                self.twin[q].start()

        def join(self, q):
            total = self.part(q, c) + self.sb[q].astype(F32)
            ka[c * 8 + q, 0:ROWS, :] = total.astype(BF16)

        def first(self):
            for r in self.twin:
                r.wait_recv()
            oz = 1 - zl
            for i, q in enumerate((y_far * 2 + oz, y_up * 2 + oz, y_down * 2 + oz)):
                self.join(q)
                self.hops[i].start()
            for q in (y_far * 2 + zl, y * 2 + oz, y_up * 2 + zl, y_down * 2 + zl, y * 2 + zl):
                self.join(q)

        def add(self, q, slots, first=0, count=ROWS):
            at = (c * 8 + q, slice(first, first + count))
            total = ka[at].astype(F32)
            for slot in slots:
                total = total + self.rb[slot, first : first + count].astype(F32)
            ka[at] = total.astype(BF16)

        def second(self):
            self.hops[0].wait_recv()
            self.add(y_far * 2 + zl, (0,))
            self.hops[3].start()
            self.hops[4].start()
            self.hops[1].wait_recv()
            self.hops[2].wait_recv()
            self.add(y * 2 + 1 - zl, (1, 2))
            self.hops[5].start()

        def third(self):
            self.hops[3].wait_recv()
            self.add(y_up * 2 + zl, (3,), 0, 64)
            self.hops[6].start()
            self.hops[4].wait_recv()
            self.add(y_down * 2 + zl, (3,), 64, 64)
            self.hops[7].start()

        def finish(self):
            for i in (5, 6, 7):
                self.hops[i].wait_recv()
            total = ka[c * 8 + y * 2 + zl, 0:ROWS].astype(F32)
            for slot in (4, 5, 6):
                total = total + self.rb[slot].astype(F32)
            return total.astype(BF16)

        def drain(self):
            for r in self.hops + self.twin:
                r.wait_send()

    grads = Scatter(sb1, rb1, s1_sem, r1_sem)
    grads.start()
    vsum = vp[c * 4 + x].astype(F32) + vsib[x].astype(F32)
    for o in range(3):
        vx[o].wait_recv()
        vsum = vsum + vrow[o].astype(F32)
    va[d] = vsum.astype(BF16)
    vals = Gather(va, ROWS, v_sem, vf_sem)
    grads.first()
    vals.start()
    grads.second()
    vals.second()
    grads.third()
    vals.third()
    gva[me_line] = grads.finish()

    gx = []
    gf = []
    for o, dx in enumerate((2, 1, 3)):
        r = remote(
            gva.at[me_line], gva.at[me_line], gx_sem.at[0, o], gx_sem.at[1, o],
            device(y, zl, c, zh, lax.rem(x + dx, 4)),
        )
        r.start()
        gx += [r]
    r = remote(gva.at[me_line], gva.at[me_line], gf_sem.at[0, 3], gf_sem.at[1, 3], sib)
    r.start()
    gf += [r]

    def take_values(q):
        take_pair(va, xb, q)

    vals.take((0, 1, 2, 3), take_values)
    vals.fourth()
    vals.take((4, 5, 6, 7), take_values)
    take_over(va, xb)

    def second_pass(t, _):
        for g in range(KVH):
            cols = slice(g * HD, (g + 1) * HD)
            grad_probs = dot_nt(xb[t, :, :, cols].reshape(KEYS, HD), gos[t, g])
            low = probs[t, g].astype(F32)
            row_dots = jnp.sum(low * grad_probs, axis=0, keepdims=True)
            grad_scores = (low * (grad_probs - row_dots)).astype(BF16)
            key_part = dot(grad_scores, qs[t, g]) * INV_ROOT
            xb[t, :, :, cols] = key_part.astype(BF16).reshape(10, SLOTS, HD)
            query_part = dot_tn(grad_scores, xa[t, :, :, cols].reshape(KEYS, HD)) * INV_ROOT
            qs[t, g] = query_part.astype(BF16)
        return 0

    lax.fori_loop(0, 4, second_pass, 0)
    for o, dx in enumerate((2, 1, 3)):
        src = c * 4 + lax.rem(x - dx + 4, 4)
        gx[o].wait_recv()
        r = remote(gva.at[src], gva.at[src], gf_sem.at[0, o], gf_sem.at[1, o], sib)
        r.start()
        gf += [r]
    for r in vx + [v_sib]:
        r.wait_send()
    lax.fori_loop(4, 6, second_pass, 0)
    for r in gf:
        r.wait_recv()

    def input_term(n, _):
        h, first = n // 2, pl.multiple_of(lax.rem(n, 2) * 256, 256)
        part = dot_nt(gva[...].reshape(1024, KVW), wm[h, pl.ds(first, 256), :])
        cols = pl.ds(pl.multiple_of(n * 256, 256), 256)
        vp[:, :, cols] = part.astype(BF16).reshape(8, ROWS, 256)
        return 0

    lax.fori_loop(0, 4, input_term, 0)
    gi_cols = [pl.ds(pl.multiple_of(h * 4096 + x * 1024 + c * HALF, HALF), HALF) for h in range(2)]
    gi_copies = []
    gi_own = []
    for o, step in enumerate(LINE_STEPS):
        tx, tc = line_at(step)
        for h in range(2):
            r = remote(
                vp.at[tc * 4 + tx, :, pl.ds(h * HALF, HALF)], gi_ref.at[:, gi_cols[h]],
                gi_sem.at[0, o * 2 + h], gi_sem.at[1, o * 2 + h], line_dev(step),
            )
            r.start()
            gi_copies += [r]
    for h in range(2):
        e = pltpu.make_async_copy(
            vp.at[me_line, :, pl.ds(h * HALF, HALF)], gi_ref.at[:, gi_cols[h]], loc_sem.at[20 + h]
        )
        e.start()
        gi_own += [e]

    for h in range(2):
        for n in range(4):
            part = dot_tn(
                li[h].reshape(1024, HALF), gva[:, :, n * 256 : (n + 1) * 256].reshape(1024, 256)
            )
            part = part.astype(BF16).reshape(8, 64, 256)
            cols = slice((n % 2) * 256, (n % 2) * 256 + 256)
            for fb in range(8):
                zt, x1, x0 = fb // 4, (fb // 2) % 2, fb % 2
                if n < 2:
                    ga[zt * 2 + x0, h * 2 + x1, :, cols] = part[fb]
                else:
                    gb[h * 2 + x1, zt * 2 + x0, :, cols] = part[fb]
    g1 = []
    for i in range(3):
        r = remote(ga.at[lax.rem(z + i + 1, 4)], ra.at[i], g1_sem.at[0, i], g1_sem.at[1, i], z_devs[i])
        r.start()
        g1 += [r]
        r = remote(
            gb.at[lax.rem(y + i + 1, 4)], rbb.at[i], g1_sem.at[0, 3 + i], g1_sem.at[1, 3 + i], y_devs[i]
        )
        r.start()
        g1 += [r]

    lax.fori_loop(6, 11, second_pass, 0)
    for r in g1:
        r.wait_recv()
    ga[z] = (
        ga[z].astype(F32) + ra[0].astype(F32) + ra[1].astype(F32) + ra[2].astype(F32)
    ).astype(BF16)
    gb[y] = (
        gb[y].astype(F32) + rbb[0].astype(F32) + rbb[1].astype(F32) + rbb[2].astype(F32)
    ).astype(BF16)

    def owners():
        for i in range(4):
            h, x1 = i // 2, i % 2
            ty, tx = 2 * h + x // 2, x1 * 2 + zl
            yield (
                in_own_line & (ty == y) & (tx == x), device(ty, lax.rem(x, 2), c, zh, tx),
                ga.at[z, i], gwa.at[y], g2s_sem.at[i], g2r_sem.at[y],
            )
            zt, x0 = i // 2, i % 2
            ty, tx = 2 * (y // 2) + x // 2, lax.rem(y, 2) * 2 + x0
            yield (
                in_own_line & (zt == zh) & (tx == x), device(ty, lax.rem(x, 2), c, zt, tx),
                gb.at[y, i], gwb.at[z], g2s_sem.at[4 + i], g2r_sem.at[4 + z],
            )

    for to_self, dev, src, dst, ssem, rsem in owners():

        @pl.when(to_self)
        def _():
            pltpu.make_async_copy(src, dst, rsem).start()

        @pl.when(jnp.logical_not(to_self))
        def _():
            remote(src, dst, ssem, rsem, dev).start()

    lax.fori_loop(11, 16, second_pass, 0)
    grads.drain()
    vals.drain()
    last = Scatter(sb2, rb2, s2_sem, r2_sem)
    last.start()
    last.first()

    q_out = []
    for g in range(KVH):
        if g == 3:
            last.second()
        if g == 6:
            last.third()
        slots = jnp.concatenate(
            [qs[:, g, h * SLOTS : (h + 1) * SLOTS, :].reshape(256, HD) for h in range(GROUP)], axis=1
        )
        va[g] = dot_tn(own_sel, slots).astype(BF16)
        e = pltpu.make_async_copy(va.at[g], gq_ref.at[:, pl.ds(g * 1024, 1024)], out_sem.at[g])
        e.start()
        q_out += [e]

    for i in range(4):
        pltpu.make_async_copy(gwa.at[i], gwa.at[i], g2r_sem.at[i]).wait()
        pltpu.make_async_copy(gwb.at[i], gwb.at[i], g2r_sem.at[4 + i]).wait()
    gw_ref[:, 0:HALF] = (gwa[0].astype(F32) + gwa[1].astype(F32)) + (gwa[2].astype(F32) + gwa[3].astype(F32))
    gw_ref[:, HALF:] = (gwb[0].astype(F32) + gwb[1].astype(F32)) + (gwb[2].astype(F32) + gwb[3].astype(F32))
    gk_ref[...] = last.finish()

    for r in gi_copies:
        r.wait()
    for e in gi_own + q_out:
        e.wait()
    for r in li_copies + [w_copy] + gx + gf + g1:
        r.wait_send()
    last.drain()
    for to_self, dev, src, dst, ssem, rsem in owners():

        @pl.when(jnp.logical_not(to_self))
        def _():
            remote(src, dst, ssem, rsem, dev).wait_send()


def shards(layer_input, queries, key_rows, grad_out, w_value, destination, seg_start):
    any_spec = pl.BlockSpec(memory_space=pl.ANY)
    vmem_spec = pl.BlockSpec(memory_space=pltpu.VMEM)
    dma = pltpu.SemaphoreType.DMA
    tokens = pltpu.VMEM
    return pl.pallas_call(
        kernel,
        out_shape=(
            jax.ShapeDtypeStruct(queries.shape, BF16),
            jax.ShapeDtypeStruct(key_rows.shape, BF16),
            jax.ShapeDtypeStruct(layer_input.shape, BF16),
            jax.ShapeDtypeStruct((64, KVW), F32),
        ),
        in_specs=[any_spec] * 5 + [vmem_spec] * 2,
        out_specs=(any_spec, vmem_spec, any_spec, vmem_spec),
        scratch_shapes=[
            tokens((RANKS, ROWS + SLOTS, KVW), BF16),
            tokens((RANKS, ROWS, KVW), BF16),
            tokens((RANKS, KVH, ROWS, HD), BF16),
            tokens((RANKS, KVH, ROWS, HD), BF16),
            tokens((RANKS, 10, SLOTS, KVW), BF16),
            tokens((RANKS, 10, SLOTS, KVW), BF16),
            tokens((RANKS, KVH, KEYS, ROWS), BF16),
            tokens((2, 8, ROWS, HALF), BF16),
            tokens((2, HALF, KVW), BF16),
            tokens((8, ROWS, KVW), BF16),
            tokens((4, ROWS, KVW), BF16),
            tokens((3, ROWS, KVW), BF16),
            tokens((8, ROWS, KVW), BF16),
            tokens((7, ROWS, KVW), BF16),
            tokens((8, ROWS, KVW), BF16),
            tokens((7, ROWS, KVW), BF16),
            tokens((8, ROWS, KVW), BF16),
            tokens((4, 4, 64, HALF), BF16),
            tokens((4, 4, 64, HALF), BF16),
            tokens((3, 4, 64, HALF), BF16),
            tokens((3, 4, 64, HALF), BF16),
            tokens((4, 64, HALF), BF16),
            tokens((4, 64, HALF), BF16),
            tokens((8, 256, 256), BF16),
            tokens((2, 256, 1024), BF16),
            tokens((RANKS, 10, SLOTS, ROWS), BF16),
            tokens((2, 256, ROWS), F32),
            tokens((RANKS, SLOTS, ROWS), F32),
            tokens((RANKS, SLOTS, ROWS), F32),
            dma((22,)),
            dma((2, 8)),
            dma((2, 8)),
            dma((2, 8)),
            dma((2, 8)),
            dma((2, 14)),
            dma((2,)),
            dma((2,)),
            dma((2, 3)),
            dma((2, 8)),
            dma((2, 8)),
            dma((2, 8)),
            dma((2, 8)),
            dma((2, 3)),
            dma((2, 4)),
            dma((2, 14)),
            dma((2, 6)),
            dma((8,)),
            dma((8,)),
            dma((8,)),
        ],
        name="packed_backward",
        compiler_params=pltpu.CompilerParams(
            collective_id=0, has_side_effects=True, vmem_limit_bytes=64 * 1024 * 1024
        ),
    )(
        layer_input, queries, key_rows, grad_out, w_value,
        destination.reshape(1, ROWS), seg_start.reshape(1, ROWS),
    )


def solution(mesh):
    both = P(("dp", "fsdp"), None)
    return jax.shard_map(
        shards,
        mesh=mesh,
        in_specs=(both, both, both, both, P("fsdp", None), P(("dp", "fsdp")), P(("dp", "fsdp"))),
        out_specs=(both, both, both, both),
        check_vma=False,
    )
```

time: 253 us -> 190 us (0.75)
  Pallas kernels: 244 us -> 182 us
    pallas_call x1, Pallas kernels: 244 us -> 182 us  [shards(): pl.pallas_call(kernel, out_shape=(jax.ShapeDtypeStruct(queries.shape, BF1...]
where the time goes in v2:
time: 190 us; the launch traced here: 189 us
  Pallas kernels  182 us (96%)
  local copies, waits for them, and re-layouts  5.98 us (3%)
    pallas_call x1, Pallas kernels, shards(): pl.pallas_call(kernel, out_shape=(jax.ShapeDtypeStruct(queries.shape, BF1...  182 us
    unnamed x10, local copies, waits for them, and re-layouts  5.98 us

profile of v2, /device:TPU:1, one launch (start us, length us, event | category | flops | bytes accessed | tf_op | source)
XLA Modules:
  0.0 188.9 jit_solution(8177660012835393196)
XLA Ops:
  0.6 182.2 %packed_backward.1 = (bf16[128,8192]{1,0:T(8,128)(2,1)}, bf16[128,1024]{1,0:T(8,128)(2,1)}, bf16[128,8192]{1,0:T(8,128)(2,1)}, f32[64,1024]{1,0:T(8,128)}) custom-call(bf16[128,8192]{1,0:T(8,128)(2,1)} %li_ref.1, bf16[128,8192]{1,0:T(8,128)(2,1)} %q_ref.1, bf16[128,1024]{1,0:T(8,128)(2,1)} %k_ref.1, bf16[128,8192]{1,0:T(8,128)(2,1)} %go_ref.1, ...), custom_call_target="tpu_custom_call" | custom-call | tf_op jit(solution)/shard_map/packed_backward/pallas_call | solution.py:630
  182.9 0.0 copy-start.2
  182.9 0.0 copy-start
  182.9 3.2 %copy.15 = bf16[128,8192]{1,0:T(8,128)(2,1)} copy(bf16[128,8192]{1,0:T(8,128)(2,1)} %get-tuple-element.8) | data formatting | bytes 4194304
  186.1 0.0 copy-done.2
  186.1 0.7 copy.16
  186.8 0.0 copy-done
  186.8 0.0 copy-start.1
  186.8 1.3 copy.17
  188.2 0.0 copy-done.1
  188.2 0.7 copy.18
Async XLA Ops:
  182.9 3.3 %copy-start.2 = (bf16[128,1024]{1,0:T(8,128)(2,1)S(1)}, bf16[128,1024]{1,0:T(8,128)(2,1)}, u32[]{:S(2)}) copy-start(bf16[128,1024]{1,0:T(8,128)(2,1)} %get-tuple-element.9) | copy-start | bytes 786436
  182.9 4.0 %copy-start = (bf16[128,8192]{1,0:T(8,128)(2,1)S(1)}, bf16[128,8192]{1,0:T(8,128)(2,1)}, u32[]{:S(2)}) copy-start(bf16[128,8192]{1,0:T(8,128)(2,1)} %get-tuple-element.10) | copy-start | bytes 6291460
  186.8 1.3 copy-start.1

commit v3 on v2

--- a/solution.py
+++ b/solution.py
@@ -288,21 +288,27 @@
     for half in range(2):
         labk[:, 8 + half] = labo[half].astype(BF16).reshape(RANKS, SLOTS, ROWS)
 
-    def first_pass(t, _):
-        marks = labk[t].reshape(KEYS, ROWS).astype(F32)
-        bias = jnp.where((marks <= posl[t][0:1]) & (marks >= startl[t][0:1]), 0.0, -1e30)
-        for g in range(KVH):
-            cols = slice(g * HD, (g + 1) * HD)
-            scores = dot_nt(xa[t, :, :, cols].reshape(KEYS, HD), qs[t, g]) * (INV_ROOT * LOG2E) + bias
-            peak = jnp.maximum(jnp.max(scores, axis=0, keepdims=True), -1e29)
-            expo = jnp.exp2(scores - peak)
-            total = jnp.maximum(jnp.sum(expo, axis=0, keepdims=True), 0.5)
-            low = (expo * (1.0 / total)).astype(BF16)
-            probs[t, g] = low
-            xb[t, :, :, cols] = dot(low, gos[t, g]).astype(BF16).reshape(10, SLOTS, HD)
-        return 0
-
-    lax.fori_loop(0, 4, first_pass, 0)
+    def first_pass(half, first, last):
+        def block_step(t, _):
+            marks = labk[t].reshape(KEYS, ROWS).astype(F32)
+            bias = jnp.where((marks <= posl[t][0:1]) & (marks >= startl[t][0:1]), 0.0, -1e30)
+            heads = range(half * 4, half * 4 + 4)
+            cols = [slice(g * HD, (g + 1) * HD) for g in heads]
+            scores = [dot_nt(xa[t, :, :, at].reshape(KEYS, HD), qs[t, g]) for g, at in zip(heads, cols)]
+            scores = [v * (INV_ROOT * LOG2E) + bias for v in scores]
+            peaks = [jnp.maximum(jnp.max(v, axis=0, keepdims=True), -1e29) for v in scores]
+            expos = [jnp.exp2(v - peak) for v, peak in zip(scores, peaks)]
+            totals = [jnp.maximum(jnp.sum(v, axis=0, keepdims=True), 0.5) for v in expos]
+            lows = [(v * (1.0 / total)).astype(BF16) for v, total in zip(expos, totals)]
+            parts = [dot(low, gos[t, g]).astype(BF16) for g, low in zip(heads, lows)]
+            for g, at, low, part in zip(heads, cols, lows, parts):
+                probs[t, g] = low
+                xb[t, :, :, at] = part.reshape(10, SLOTS, HD)
+            return 0
+
+        lax.fori_loop(first, last, block_step, 0)
+
+    first_pass(0, 0, 6)
 
     for e in li_own:
         e.wait()
@@ -325,7 +331,7 @@
     v_sib = remote(vp.at[pl.ds((1 - c) * 4, 4)], vsib, vs_sem.at[0], vs_sem.at[1], sib)
     v_sib.start()
     value_term(c)
-    lax.fori_loop(4, 6, first_pass, 0)
+    first_pass(0, 6, 16)
 
     v_sib.wait_recv()
     vx = []
@@ -339,14 +345,19 @@
         )
         r.start()
         vx += [r]
-    lax.fori_loop(6, 16, first_pass, 0)
     keys.drain()
 
     class Scatter:
-        def __init__(self, sb, rb, ssems, rsems):
+        def __init__(self, half, sb, rb, ssems, rsems):
             self.sb, self.rb = sb, rb
+            self.cols = slice(half * HALF, (half + 1) * HALF)
+            lanes = pl.ds(half * HALF, HALF)
+            base = half * 2
             self.twin = [
-                remote(self.block(q, 1 - c), sb.at[q], ssems.at[0, q], ssems.at[1, q], sib)
+                remote(
+                    ka.at[(1 - c) * 8 + q, pl.ds(0, ROWS), lanes], sb.at[q, :, lanes],
+                    ssems.at[base, q], ssems.at[base + 1, q], sib,
+                )
                 for q in range(8)
             ]
             oz = 1 - zl
@@ -359,30 +370,29 @@
             )
             self.hops = [
                 remote(
-                    ka.at[c * 8 + q, pl.ds(first, count)], rb.at[slot, pl.ds(first, count)],
-                    rsems.at[0, i], rsems.at[1, i], dev,
+                    ka.at[c * 8 + q, pl.ds(first, count), lanes],
+                    rb.at[slot, pl.ds(first, count), lanes],
+                    rsems.at[base, i], rsems.at[base + 1, i], dev,
                 )
                 for i, (q, slot, first, count, dev) in enumerate(plan)
             ]
 
-        def block(self, q, core):
-            return ka.at[core * 8 + q, pl.ds(0, ROWS)]
-
         def part(self, q, core):
             s = q * 2 + core
             lanes = pl.ds(pl.multiple_of(core * ROWS, ROWS), ROWS)
-            total = dot_tn(sel[q, :, lanes], xb[:, q].reshape(256, KVW))
+            total = dot_tn(sel[q, :, lanes], xb[:, q, :, self.cols].reshape(256, HALF))
             lanes = pl.ds(pl.multiple_of(lax.rem(s, 8) * ROWS, ROWS), ROWS)
-            return total + dot_tn(selo[s // 8, :, lanes], xb[:, 8 + s // 8].reshape(256, KVW))
+            rows = xb[:, 8 + s // 8, :, self.cols].reshape(256, HALF)
+            return total + dot_tn(selo[s // 8, :, lanes], rows)
 
         def start(self):
             for q in range(8):
-                ka[(1 - c) * 8 + q, 0:ROWS, :] = self.part(q, 1 - c).astype(BF16)
+                ka[(1 - c) * 8 + q, 0:ROWS, self.cols] = self.part(q, 1 - c).astype(BF16)
                 self.twin[q].start()
 
         def join(self, q):
-            total = self.part(q, c) + self.sb[q].astype(F32)
-            ka[c * 8 + q, 0:ROWS, :] = total.astype(BF16)
+            total = self.part(q, c) + self.sb[q, :, self.cols].astype(F32)
+            ka[c * 8 + q, 0:ROWS, self.cols] = total.astype(BF16)
 
         def first(self):
             for r in self.twin:
@@ -395,10 +405,10 @@
                 self.join(q)
 
         def add(self, q, slots, first=0, count=ROWS):
-            at = (c * 8 + q, slice(first, first + count))
+            at = (c * 8 + q, slice(first, first + count), self.cols)
             total = ka[at].astype(F32)
             for slot in slots:
-                total = total + self.rb[slot, first : first + count].astype(F32)
+                total = total + self.rb[slot, first : first + count, self.cols].astype(F32)
             ka[at] = total.astype(BF16)
 
         def second(self):
@@ -422,30 +432,39 @@
         def finish(self):
             for i in (5, 6, 7):
                 self.hops[i].wait_recv()
-            total = ka[c * 8 + y * 2 + zl, 0:ROWS].astype(F32)
+            total = ka[c * 8 + y * 2 + zl, 0:ROWS, self.cols].astype(F32)
             for slot in (4, 5, 6):
-                total = total + self.rb[slot].astype(F32)
+                total = total + self.rb[slot, :, self.cols].astype(F32)
             return total.astype(BF16)
 
         def drain(self):
             for r in self.hops + self.twin:
                 r.wait_send()
 
-    grads = Scatter(sb1, rb1, s1_sem, r1_sem)
-    grads.start()
+    left = Scatter(0, sb1, rb1, s1_sem, r1_sem)
+    right = Scatter(1, sb1, rb1, s1_sem, r1_sem)
+    left.start()
+    first_pass(1, 0, 6)
+    left.first()
+    first_pass(1, 6, 12)
+    left.second()
     vsum = vp[c * 4 + x].astype(F32) + vsib[x].astype(F32)
     for o in range(3):
         vx[o].wait_recv()
         vsum = vsum + vrow[o].astype(F32)
     va[d] = vsum.astype(BF16)
     vals = Gather(va, ROWS, v_sem, vf_sem)
-    grads.first()
     vals.start()
-    grads.second()
+    first_pass(1, 12, 16)
+    left.third()
+    right.start()
     vals.second()
-    grads.third()
+    right.first()
+    gva[me_line, :, 0:HALF] = left.finish()
     vals.third()
-    gva[me_line] = grads.finish()
+    right.second()
+    right.third()
+    gva[me_line, :, HALF:] = right.finish()
 
     gx = []
     gf = []
@@ -468,20 +487,29 @@
     vals.take((4, 5, 6, 7), take_values)
     take_over(va, xb)
 
-    def second_pass(t, _):
-        for g in range(KVH):
-            cols = slice(g * HD, (g + 1) * HD)
-            grad_probs = dot_nt(xb[t, :, :, cols].reshape(KEYS, HD), gos[t, g])
-            low = probs[t, g].astype(F32)
-            row_dots = jnp.sum(low * grad_probs, axis=0, keepdims=True)
-            grad_scores = (low * (grad_probs - row_dots)).astype(BF16)
-            key_part = dot(grad_scores, qs[t, g]) * INV_ROOT
-            xb[t, :, :, cols] = key_part.astype(BF16).reshape(10, SLOTS, HD)
-            query_part = dot_tn(grad_scores, xa[t, :, :, cols].reshape(KEYS, HD)) * INV_ROOT
-            qs[t, g] = query_part.astype(BF16)
-        return 0
-
-    lax.fori_loop(0, 4, second_pass, 0)
+    def second_pass(half, first, last):
+        def block_step(t, _):
+            heads = range(half * 4, half * 4 + 4)
+            cols = [slice(g * HD, (g + 1) * HD) for g in heads]
+            grad_probs = [dot_nt(xb[t, :, :, at].reshape(KEYS, HD), gos[t, g]) for g, at in zip(heads, cols)]
+            lows = [probs[t, g].astype(F32) for g in heads]
+            row_dots = [jnp.sum(low * v, axis=0, keepdims=True) for low, v in zip(lows, grad_probs)]
+            grad_scores = [
+                (low * (v - dots)).astype(BF16) for low, v, dots in zip(lows, grad_probs, row_dots)
+            ]
+            key_parts = [dot(v, qs[t, g]) * INV_ROOT for v, g in zip(grad_scores, heads)]
+            query_parts = [
+                dot_tn(v, xa[t, :, :, at].reshape(KEYS, HD)) * INV_ROOT
+                for v, at in zip(grad_scores, cols)
+            ]
+            for g, at, key_part, query_part in zip(heads, cols, key_parts, query_parts):
+                xb[t, :, :, at] = key_part.astype(BF16).reshape(10, SLOTS, HD)
+                qs[t, g] = query_part.astype(BF16)
+            return 0
+
+        lax.fori_loop(first, last, block_step, 0)
+
+    second_pass(0, 0, 8)
     for o, dx in enumerate((2, 1, 3)):
         src = c * 4 + lax.rem(x - dx + 4, 4)
         gx[o].wait_recv()
@@ -490,7 +518,12 @@
         gf += [r]
     for r in vx + [v_sib]:
         r.wait_send()
-    lax.fori_loop(4, 6, second_pass, 0)
+    second_pass(0, 8, 16)
+    left.drain()
+    right.drain()
+    last_left = Scatter(0, sb2, rb2, s2_sem, r2_sem)
+    last_right = Scatter(1, sb2, rb2, s2_sem, r2_sem)
+    last_left.start()
     for r in gf:
         r.wait_recv()
 
@@ -520,6 +553,8 @@
         )
         e.start()
         gi_own += [e]
+
+    last_left.first()
 
     for h in range(2):
         for n in range(4):
@@ -545,7 +580,10 @@
         r.start()
         g1 += [r]
 
-    lax.fori_loop(6, 11, second_pass, 0)
+    second_pass(1, 0, 6)
+    last_left.second()
+    second_pass(1, 6, 12)
+    last_left.third()
     for r in g1:
         r.wait_recv()
     ga[z] = (
@@ -580,33 +618,35 @@
         def _():
             remote(src, dst, ssem, rsem, dev).start()
 
-    lax.fori_loop(11, 16, second_pass, 0)
-    grads.drain()
+    second_pass(1, 12, 16)
+    last_right.start()
     vals.drain()
-    last = Scatter(sb2, rb2, s2_sem, r2_sem)
-    last.start()
-    last.first()
 
     q_out = []
-    for g in range(KVH):
-        if g == 3:
-            last.second()
-        if g == 6:
-            last.third()
+
+    def queries_out(g):
         slots = jnp.concatenate(
             [qs[:, g, h * SLOTS : (h + 1) * SLOTS, :].reshape(256, HD) for h in range(GROUP)], axis=1
         )
         va[g] = dot_tn(own_sel, slots).astype(BF16)
         e = pltpu.make_async_copy(va.at[g], gq_ref.at[:, pl.ds(g * 1024, 1024)], out_sem.at[g])
         e.start()
-        q_out += [e]
-
+        q_out.append(e)
+
+    for g in range(6):
+        queries_out(g)
+    last_right.first()
+    gk_ref[:, 0:HALF] = last_left.finish()
+    queries_out(6)
+    queries_out(7)
+    last_right.second()
+    last_right.third()
     for i in range(4):
         pltpu.make_async_copy(gwa.at[i], gwa.at[i], g2r_sem.at[i]).wait()
         pltpu.make_async_copy(gwb.at[i], gwb.at[i], g2r_sem.at[4 + i]).wait()
     gw_ref[:, 0:HALF] = (gwa[0].astype(F32) + gwa[1].astype(F32)) + (gwa[2].astype(F32) + gwa[3].astype(F32))
     gw_ref[:, HALF:] = (gwb[0].astype(F32) + gwb[1].astype(F32)) + (gwb[2].astype(F32) + gwb[3].astype(F32))
-    gk_ref[...] = last.finish()
+    gk_ref[:, HALF:] = last_right.finish()
 
     for r in gi_copies:
         r.wait()
@@ -614,7 +654,8 @@
         e.wait()
     for r in li_copies + [w_copy] + gx + gf + g1:
         r.wait_send()
-    last.drain()
+    last_left.drain()
+    last_right.drain()
     for to_self, dev, src, dst, ssem, rsem in owners():
 
         @pl.when(jnp.logical_not(to_self))
@@ -676,10 +717,10 @@
             dma((2,)),
             dma((2,)),
             dma((2, 3)),
-            dma((2, 8)),
-            dma((2, 8)),
-            dma((2, 8)),
-            dma((2, 8)),
+            dma((4, 8)),
+            dma((4, 8)),
+            dma((4, 8)),
+            dma((4, 8)),
             dma((2, 3)),
             dma((2, 4)),
             dma((2, 14)),

time: 190 us -> 166 us (0.87)
  Pallas kernels: 182 us -> 158 us
    pallas_call x1, Pallas kernels: 182 us -> 158 us  [shards(): pl.pallas_call(kernel, out_shape=(jax.ShapeDtypeStruct(queries.shape, BF1...]
where the time goes in v3:
time: 166 us; the launch traced here: 165 us
  Pallas kernels  158 us (95%)
  local copies, waits for them, and re-layouts  5.98 us (4%)
    pallas_call x1, Pallas kernels, shards(): pl.pallas_call(kernel, out_shape=(jax.ShapeDtypeStruct(queries.shape, BF1...  158 us
    unnamed x10, local copies, waits for them, and re-layouts  5.98 us

profile of v3, /device:TPU:1, one launch (start us, length us, event | category | flops | bytes accessed | tf_op | source)
XLA Modules:
  0.0 164.6 jit_solution(3484923058285870363)
XLA Ops:
  0.6 158.0 %packed_backward.1 = (bf16[128,8192]{1,0:T(8,128)(2,1)}, bf16[128,1024]{1,0:T(8,128)(2,1)}, bf16[128,8192]{1,0:T(8,128)(2,1)}, f32[64,1024]{1,0:T(8,128)}) custom-call(bf16[128,8192]{1,0:T(8,128)(2,1)} %li_ref.1, bf16[128,8192]{1,0:T(8,128)(2,1)} %q_ref.1, bf16[128,1024]{1,0:T(8,128)(2,1)} %k_ref.1, bf16[128,8192]{1,0:T(8,128)(2,1)} %go_ref.1, ...), custom_call_target="tpu_custom_call" | custom-call | tf_op jit(solution)/shard_map/packed_backward/pallas_call | solution.py:671
  158.6 0.0 copy-start.2
  158.6 0.0 copy-start
  158.6 3.2 %copy.15 = bf16[128,8192]{1,0:T(8,128)(2,1)} copy(bf16[128,8192]{1,0:T(8,128)(2,1)} %get-tuple-element.8) | data formatting | bytes 4194304
  161.9 0.0 copy-done.2
  161.9 0.7 copy.16
  162.6 0.0 copy-done
  162.6 0.0 copy-start.1
  162.6 1.3 copy.17
  163.9 0.0 copy-done.1
  163.9 0.7 copy.18
Async XLA Ops:
  158.6 3.3 %copy-start.2 = (bf16[128,1024]{1,0:T(8,128)(2,1)S(1)}, bf16[128,1024]{1,0:T(8,128)(2,1)}, u32[]{:S(2)}) copy-start(bf16[128,1024]{1,0:T(8,128)(2,1)} %get-tuple-element.9) | copy-start | bytes 786436
  158.6 4.0 %copy-start = (bf16[128,8192]{1,0:T(8,128)(2,1)S(1)}, bf16[128,8192]{1,0:T(8,128)(2,1)}, u32[]{:S(2)}) copy-start(bf16[128,8192]{1,0:T(8,128)(2,1)} %get-tuple-element.10) | copy-start | bytes 6291460
  162.6 1.3 copy-start.1

commit v4 on v3

--- a/solution.py
+++ b/solution.py
@@ -129,15 +129,15 @@
     own_k.wait()
 
     class Gather:
-        def __init__(self, buf, rows, sems, fsems):
+        def __init__(self, buf, rows, sems, fsems, base=0, lanes=pl.ds(0, KVW)):
             chips = [(y, zl), (y, 1 - zl), (y_down, zl), (y_up, zl)]
             chips += [(y_down, 1 - zl), (y_up, 1 - zl), (y_far, zl), (y_far, 1 - zl)]
             self.q = [cy * 2 + cz for cy, cz in chips]
             me, zs, yd, yu, _, _, yo, _ = [q * 2 + c for q in self.q]
 
             def hop(i, slot, dev, first=0, count=rows):
-                part = buf.at[slot, pl.ds(first, count)]
-                return remote(part, part, sems.at[0, i], sems.at[1, i], dev)
+                part = buf.at[slot, pl.ds(first, count), lanes]
+                return remote(part, part, sems.at[base, i], sems.at[base + 1, i], dev)
 
             self.hops = [
                 hop(0, me, dev_up), hop(1, me, dev_down), hop(2, me, dev_z),
@@ -146,7 +146,10 @@
                 hop(7, yo, dev_z),
             ]
             self.twin = [
-                remote(buf.at[q * 2 + c], buf.at[q * 2 + c], fsems.at[0, j], fsems.at[1, j], sib)
+                remote(
+                    buf.at[q * 2 + c, pl.ds(0, rows), lanes], buf.at[q * 2 + c, pl.ds(0, rows), lanes],
+                    fsems.at[base, j], fsems.at[base + 1, j], sib,
+                )
                 for j, q in enumerate(self.q)
             ]
 
@@ -190,8 +193,12 @@
             for r in self.hops + self.twin:
                 r.wait_send()
 
-    keys = Gather(ka, ROWS + SLOTS, k_sem, kf_sem)
-    keys.start()
+    keys = [
+        Gather(ka, ROWS + SLOTS * (1 - half), k_sem, kf_sem, half * 2, pl.ds(half * HALF, HALF))
+        for half in range(2)
+    ]
+    keys[0].start()
+    keys[1].start()
     li_copies = []
     for o, step in enumerate(LINE_STEPS):
         tx, tc = line_at(step)
@@ -237,10 +244,12 @@
         q_loads[g].wait()
         by_block(g, qs)
         go_loads += [load(go_ref, g, loc_sem.at[9 + g])]
-    keys.second()
+    keys[0].second()
     for g in range(KVH):
         go_loads[g].wait()
         by_block(g, gos)
+    keys[1].second()
+    keys[0].third()
 
     def take_keys(q):
         for core in range(2):
@@ -267,24 +276,23 @@
             posl[s] = dot_nt(label.astype(BF16), mine.astype(BF16))
             startl[s] = dot_nt(seg_s.astype(BF16), at_row) + 1.0
         labk[:, q] = marks.astype(BF16).reshape(RANKS, SLOTS, ROWS)
-        take_pair(ka, xa, q)
-
-    def take_pair(buf, dst, q):
-        pair = buf[pl.ds(q * 2, 2), 0:ROWS, :].reshape(2 * ROWS, KVW)
-        dst[:, q] = dot(sel[q], pair).astype(BF16).reshape(RANKS, SLOTS, KVW)
-
-    def take_over(buf, dst):
-        for half in range(2):
-            rows = buf[half * 8 : half * 8 + 8, 0:ROWS, :].reshape(8 * ROWS, KVW)
-            dst[:, 8 + half] = dot(selo[half], rows).astype(BF16).reshape(RANKS, SLOTS, KVW)
+        take_pair(ka, xa, q, slice(0, HALF))
+
+    def take_pair(buf, dst, q, cols=slice(0, KVW)):
+        pair = buf[pl.ds(q * 2, 2), 0:ROWS, cols].reshape(2 * ROWS, -1)
+        dst[:, q, :, cols] = dot(sel[q], pair).astype(BF16).reshape(RANKS, SLOTS, -1)
+
+    def take_over(buf, dst, cols=slice(0, KVW)):
+        for part in range(2):
+            rows = buf[part * 8 : part * 8 + 8, 0:ROWS, cols].reshape(8 * ROWS, -1)
+            dst[:, 8 + part, :, cols] = dot(selo[part], rows).astype(BF16).reshape(RANKS, SLOTS, -1)
 
     labo[...] = jnp.zeros_like(labo)
-    keys.take((0,), take_keys)
-    keys.third()
-    keys.take((1, 2, 3), take_keys)
-    keys.fourth()
-    keys.take((4, 5, 6, 7), take_keys)
-    take_over(ka, xa)
+    keys[0].take((0, 1, 2, 3), take_keys)
+    keys[0].fourth()
+    keys[1].third()
+    keys[0].take((4, 5, 6, 7), take_keys)
+    take_over(ka, xa, slice(0, HALF))
     for half in range(2):
         labk[:, 8 + half] = labo[half].astype(BF16).reshape(RANKS, SLOTS, ROWS)
 
@@ -308,7 +316,8 @@
 
         lax.fori_loop(first, last, block_step, 0)
 
-    first_pass(0, 0, 6)
+    keys[1].fourth()
+    first_pass(0, 0, 16)
 
     for e in li_own:
         e.wait()
@@ -331,7 +340,9 @@
     v_sib = remote(vp.at[pl.ds((1 - c) * 4, 4)], vsib, vs_sem.at[0], vs_sem.at[1], sib)
     v_sib.start()
     value_term(c)
-    first_pass(0, 6, 16)
+    right_cols = slice(HALF, KVW)
+    keys[1].take(range(8), lambda q: take_pair(ka, xa, q, right_cols))
+    take_over(ka, xa, right_cols)
 
     v_sib.wait_recv()
     vx = []
@@ -345,7 +356,8 @@
         )
         r.start()
         vx += [r]
-    keys.drain()
+    keys[0].drain()
+    keys[1].drain()
 
     class Scatter:
         def __init__(self, half, sb, rb, ssems, rsems):
@@ -453,39 +465,51 @@
         vx[o].wait_recv()
         vsum = vsum + vrow[o].astype(F32)
     va[d] = vsum.astype(BF16)
-    vals = Gather(va, ROWS, v_sem, vf_sem)
-    vals.start()
+    vals = [
+        Gather(va, ROWS, v_sem, vf_sem, half * 2, pl.ds(half * HALF, HALF)) for half in range(2)
+    ]
+
+    gx = [[], []]
+    gf = [[], []]
+
+    def grad_hop(half, slot, sems, i, dev):
+        part = gva.at[slot, :, pl.ds(half * HALF, HALF)]
+        r = remote(part, part, sems.at[half * 2, i], sems.at[half * 2 + 1, i], dev)
+        r.start()
+        return r
+
+    def grads_out(half, total):
+        gva[me_line, :, half * HALF : (half + 1) * HALF] = total
+        for o, dx in enumerate((2, 1, 3)):
+            gx[half] += [grad_hop(half, me_line, gx_sem, o, device(y, zl, c, zh, lax.rem(x + dx, 4)))]
+        gf[half] += [grad_hop(half, me_line, gf_sem, 3, sib)]
+
+    def grads_on(half):
+        for o, dx in enumerate((2, 1, 3)):
+            gx[half][o].wait_recv()
+            gf[half] += [grad_hop(half, c * 4 + lax.rem(x - dx + 4, 4), gf_sem, o, sib)]
+
+    def take_values(half):
+        cols = slice(half * HALF, (half + 1) * HALF)
+        vals[half].take(range(8), lambda q: take_pair(va, xb, q, cols))
+        take_over(va, xb, cols)
+
+    vals[0].start()
     first_pass(1, 12, 16)
     left.third()
     right.start()
-    vals.second()
+    vals[0].second()
+    vals[1].start()
     right.first()
-    gva[me_line, :, 0:HALF] = left.finish()
-    vals.third()
+    grads_out(0, left.finish())
+    vals[0].third()
     right.second()
+    vals[1].second()
+    vals[0].fourth()
     right.third()
-    gva[me_line, :, HALF:] = right.finish()
-
-    gx = []
-    gf = []
-    for o, dx in enumerate((2, 1, 3)):
-        r = remote(
-            gva.at[me_line], gva.at[me_line], gx_sem.at[0, o], gx_sem.at[1, o],
-            device(y, zl, c, zh, lax.rem(x + dx, 4)),
-        )
-        r.start()
-        gx += [r]
-    r = remote(gva.at[me_line], gva.at[me_line], gf_sem.at[0, 3], gf_sem.at[1, 3], sib)
-    r.start()
-    gf += [r]
-
-    def take_values(q):
-        take_pair(va, xb, q)
-
-    vals.take((0, 1, 2, 3), take_values)
-    vals.fourth()
-    vals.take((4, 5, 6, 7), take_values)
-    take_over(va, xb)
+    vals[1].third()
+    grads_out(1, right.finish())
+    take_values(0)
 
     def second_pass(half, first, last):
         def block_step(t, _):
@@ -510,21 +534,20 @@
         lax.fori_loop(first, last, block_step, 0)
 
     second_pass(0, 0, 8)
-    for o, dx in enumerate((2, 1, 3)):
-        src = c * 4 + lax.rem(x - dx + 4, 4)
-        gx[o].wait_recv()
-        r = remote(gva.at[src], gva.at[src], gf_sem.at[0, o], gf_sem.at[1, o], sib)
-        r.start()
-        gf += [r]
-    for r in vx + [v_sib]:
-        r.wait_send()
+    vals[1].fourth()
+    grads_on(0)
     second_pass(0, 8, 16)
     left.drain()
     right.drain()
     last_left = Scatter(0, sb2, rb2, s2_sem, r2_sem)
     last_right = Scatter(1, sb2, rb2, s2_sem, r2_sem)
     last_left.start()
-    for r in gf:
+    grads_on(1)
+    take_values(1)
+    last_left.first()
+    for r in vx + [v_sib]:
+        r.wait_send()
+    for r in gf[0] + gf[1]:
         r.wait_recv()
 
     def input_term(n, _):
@@ -534,27 +557,24 @@
         vp[:, :, cols] = part.astype(BF16).reshape(8, ROWS, 256)
         return 0
 
-    lax.fori_loop(0, 4, input_term, 0)
-    gi_cols = [pl.ds(pl.multiple_of(h * 4096 + x * 1024 + c * HALF, HALF), HALF) for h in range(2)]
     gi_copies = []
     gi_own = []
-    for o, step in enumerate(LINE_STEPS):
-        tx, tc = line_at(step)
-        for h in range(2):
+    for h in range(2):
+        lax.fori_loop(h * 2, h * 2 + 2, input_term, 0)
+        gi_cols = pl.ds(pl.multiple_of(h * 4096 + x * 1024 + c * HALF, HALF), HALF)
+        for o, step in enumerate(LINE_STEPS):
+            tx, tc = line_at(step)
             r = remote(
-                vp.at[tc * 4 + tx, :, pl.ds(h * HALF, HALF)], gi_ref.at[:, gi_cols[h]],
+                vp.at[tc * 4 + tx, :, pl.ds(h * HALF, HALF)], gi_ref.at[:, gi_cols],
                 gi_sem.at[0, o * 2 + h], gi_sem.at[1, o * 2 + h], line_dev(step),
             )
             r.start()
             gi_copies += [r]
-    for h in range(2):
         e = pltpu.make_async_copy(
-            vp.at[me_line, :, pl.ds(h * HALF, HALF)], gi_ref.at[:, gi_cols[h]], loc_sem.at[20 + h]
+            vp.at[me_line, :, pl.ds(h * HALF, HALF)], gi_ref.at[:, gi_cols], loc_sem.at[20 + h]
         )
         e.start()
         gi_own += [e]
-
-    last_left.first()
 
     for h in range(2):
         for n in range(4):
@@ -580,10 +600,29 @@
         r.start()
         g1 += [r]
 
-    second_pass(1, 0, 6)
     last_left.second()
-    second_pass(1, 6, 12)
+    second_pass(1, 0, 8)
     last_left.third()
+    second_pass(1, 8, 16)
+    last_right.start()
+    for v in vals:
+        v.drain()
+
+    q_out = []
+
+    def queries_out(g):
+        slots = jnp.concatenate(
+            [qs[:, g, h * SLOTS : (h + 1) * SLOTS, :].reshape(256, HD) for h in range(GROUP)], axis=1
+        )
+        va[g] = dot_tn(own_sel, slots).astype(BF16)
+        e = pltpu.make_async_copy(va.at[g], gq_ref.at[:, pl.ds(g * 1024, 1024)], out_sem.at[g])
+        e.start()
+        q_out.append(e)
+
+    for g in range(4):
+        queries_out(g)
+    last_right.first()
+    gk_ref[:, 0:HALF] = last_left.finish()
     for r in g1:
         r.wait_recv()
     ga[z] = (
@@ -618,27 +657,8 @@
         def _():
             remote(src, dst, ssem, rsem, dev).start()
 
-    second_pass(1, 12, 16)
-    last_right.start()
-    vals.drain()
-
-    q_out = []
-
-    def queries_out(g):
-        slots = jnp.concatenate(
-            [qs[:, g, h * SLOTS : (h + 1) * SLOTS, :].reshape(256, HD) for h in range(GROUP)], axis=1
-        )
-        va[g] = dot_tn(own_sel, slots).astype(BF16)
-        e = pltpu.make_async_copy(va.at[g], gq_ref.at[:, pl.ds(g * 1024, 1024)], out_sem.at[g])
-        e.start()
-        q_out.append(e)
-
-    for g in range(6):
+    for g in range(4, KVH):
         queries_out(g)
-    last_right.first()
-    gk_ref[:, 0:HALF] = last_left.finish()
-    queries_out(6)
-    queries_out(7)
     last_right.second()
     last_right.third()
     for i in range(4):
@@ -652,7 +672,7 @@
         r.wait()
     for e in gi_own + q_out:
         e.wait()
-    for r in li_copies + [w_copy] + gx + gf + g1:
+    for r in li_copies + [w_copy] + gx[0] + gx[1] + gf[0] + gf[1] + g1:
         r.wait_send()
     last_left.drain()
     last_right.drain()
@@ -709,10 +729,10 @@
             tokens((RANKS, SLOTS, ROWS), F32),
             tokens((RANKS, SLOTS, ROWS), F32),
             dma((22,)),
-            dma((2, 8)),
-            dma((2, 8)),
-            dma((2, 8)),
-            dma((2, 8)),
+            dma((4, 8)),
+            dma((4, 8)),
+            dma((4, 8)),
+            dma((4, 8)),
             dma((2, 14)),
             dma((2,)),
             dma((2,)),
@@ -721,8 +741,8 @@
             dma((4, 8)),
             dma((4, 8)),
             dma((4, 8)),
-            dma((2, 3)),
-            dma((2, 4)),
+            dma((4, 3)),
+            dma((4, 4)),
             dma((2, 14)),
             dma((2, 6)),
             dma((8,)),

time: 166 us -> 161 us (0.970)
  Pallas kernels: 158 us -> 154 us
    pallas_call x1, Pallas kernels: 158 us -> 154 us  [shards(): pl.pallas_call(kernel, out_shape=(jax.ShapeDtypeStruct(queries.shape, BF1...]
where the time goes in v4:
time: 161 us
  Pallas kernels  154 us (96%)
  local copies, waits for them, and re-layouts  5.98 us (4%)
    pallas_call x1, Pallas kernels, shards(): pl.pallas_call(kernel, out_shape=(jax.ShapeDtypeStruct(queries.shape, BF1...  154 us
    unnamed x10, local copies, waits for them, and re-layouts  5.98 us

profile of v4, /device:TPU:1, one launch (start us, length us, event | category | flops | bytes accessed | tf_op | source)
XLA Modules:
  0.0 161.0 jit_solution(9850756507581056466)
XLA Ops:
  0.6 154.3 %packed_backward.1 = (bf16[128,8192]{1,0:T(8,128)(2,1)}, bf16[128,1024]{1,0:T(8,128)(2,1)}, bf16[128,8192]{1,0:T(8,128)(2,1)}, f32[64,1024]{1,0:T(8,128)}) custom-call(bf16[128,8192]{1,0:T(8,128)(2,1)} %li_ref.1, bf16[128,8192]{1,0:T(8,128)(2,1)} %q_ref.1, bf16[128,1024]{1,0:T(8,128)(2,1)} %k_ref.1, bf16[128,8192]{1,0:T(8,128)(2,1)} %go_ref.1, ...), custom_call_target="tpu_custom_call" | custom-call | tf_op jit(solution)/shard_map/packed_backward/pallas_call | solution.py:691
  155.0 0.0 copy-start.2
  155.0 0.0 copy-start
  155.0 3.2 %copy.15 = bf16[128,8192]{1,0:T(8,128)(2,1)} copy(bf16[128,8192]{1,0:T(8,128)(2,1)} %get-tuple-element.8) | data formatting | bytes 4194304
  158.2 0.0 copy-done.2
  158.2 0.7 copy.16
  158.9 0.0 copy-done
  158.9 0.0 copy-start.1
  158.9 1.3 copy.17
  160.2 0.0 copy-done.1
  160.2 0.7 copy.18
Async XLA Ops:
  155.0 3.3 %copy-start.2 = (bf16[128,1024]{1,0:T(8,128)(2,1)S(1)}, bf16[128,1024]{1,0:T(8,128)(2,1)}, u32[]{:S(2)}) copy-start(bf16[128,1024]{1,0:T(8,128)(2,1)} %get-tuple-element.9) | copy-start | bytes 786436
  155.0 4.0 %copy-start = (bf16[128,8192]{1,0:T(8,128)(2,1)S(1)}, bf16[128,8192]{1,0:T(8,128)(2,1)}, u32[]{:S(2)}) copy-start(bf16[128,8192]{1,0:T(8,128)(2,1)} %get-tuple-element.10) | copy-start | bytes 6291460
  158.9 1.3 copy-start.1

commit v5 on v4

--- a/solution.py
+++ b/solution.py
@@ -345,17 +345,20 @@
     take_over(ka, xa, right_cols)
 
     v_sib.wait_recv()
-    vx = []
-    own_v = None
-    for o, dx in enumerate((2, 1, 3)):
-        tx = lax.rem(x + dx, 4)
-        vp[c * 4 + tx] = (vp[c * 4 + tx].astype(F32) + vsib[tx].astype(F32)).astype(BF16)
-        r = remote(
-            vp.at[c * 4 + tx], vrow.at[o], vx_sem.at[0, o], vx_sem.at[1, o],
-            device(y, zl, c, zh, tx),
-        )
-        r.start()
-        vx += [r]
+    vx = [[], []]
+    for half in range(2):
+        cols = slice(half * HALF, (half + 1) * HALF)
+        for o, dx in enumerate((2, 1, 3)):
+            tx = lax.rem(x + dx, 4)
+            total = vp[c * 4 + tx, :, cols].astype(F32) + vsib[tx, :, cols].astype(F32)
+            vp[c * 4 + tx, :, cols] = total.astype(BF16)
+            lanes = pl.ds(half * HALF, HALF)
+            r = remote(
+                vp.at[c * 4 + tx, :, lanes], vrow.at[o, :, lanes],
+                vx_sem.at[half * 2, o], vx_sem.at[half * 2 + 1, o], device(y, zl, c, zh, tx),
+            )
+            r.start()
+            vx[half] += [r]
     keys[0].drain()
     keys[1].drain()
 
@@ -460,11 +463,14 @@
     left.first()
     first_pass(1, 6, 12)
     left.second()
-    vsum = vp[c * 4 + x].astype(F32) + vsib[x].astype(F32)
-    for o in range(3):
-        vx[o].wait_recv()
-        vsum = vsum + vrow[o].astype(F32)
-    va[d] = vsum.astype(BF16)
+    def own_values(half):
+        cols = slice(half * HALF, (half + 1) * HALF)
+        total = vp[c * 4 + x, :, cols].astype(F32) + vsib[x, :, cols].astype(F32)
+        for o in range(3):
+            vx[half][o].wait_recv()
+            total = total + vrow[o, :, cols].astype(F32)
+        va[d, :, cols] = total.astype(BF16)
+
     vals = [
         Gather(va, ROWS, v_sem, vf_sem, half * 2, pl.ds(half * HALF, HALF)) for half in range(2)
     ]
@@ -494,11 +500,13 @@
         vals[half].take(range(8), lambda q: take_pair(va, xb, q, cols))
         take_over(va, xb, cols)
 
+    own_values(0)
     vals[0].start()
     first_pass(1, 12, 16)
     left.third()
     right.start()
     vals[0].second()
+    own_values(1)
     vals[1].start()
     right.first()
     grads_out(0, left.finish())
@@ -545,7 +553,7 @@
     grads_on(1)
     take_values(1)
     last_left.first()
-    for r in vx + [v_sib]:
+    for r in vx[0] + vx[1] + [v_sib]:
         r.wait_send()
     for r in gf[0] + gf[1]:
         r.wait_recv()
@@ -736,7 +744,7 @@
             dma((2, 14)),
             dma((2,)),
             dma((2,)),
-            dma((2, 3)),
+            dma((4, 3)),
             dma((4, 8)),
             dma((4, 8)),
             dma((4, 8)),

time: 161 us -> 159 us (0.988)
  Pallas kernels: 154 us -> 152 us
    pallas_call x1, Pallas kernels: 154 us -> 152 us  [shards(): pl.pallas_call(kernel, out_shape=(jax.ShapeDtypeStruct(queries.shape, BF1...]
where the time goes in v5:
time: 159 us
  Pallas kernels  152 us (96%)
  local copies, waits for them, and re-layouts  5.98 us (4%)
    pallas_call x1, Pallas kernels, shards(): pl.pallas_call(kernel, out_shape=(jax.ShapeDtypeStruct(queries.shape, BF1...  152 us
    unnamed x10, local copies, waits for them, and re-layouts  5.98 us

profile of v5, /device:TPU:1, one launch (start us, length us, event | category | flops | bytes accessed | tf_op | source)
XLA Modules:
  0.0 158.5 jit_solution(11098086505658751643)
XLA Ops:
  0.6 151.9 %packed_backward.1 = (bf16[128,8192]{1,0:T(8,128)(2,1)}, bf16[128,1024]{1,0:T(8,128)(2,1)}, bf16[128,8192]{1,0:T(8,128)(2,1)}, f32[64,1024]{1,0:T(8,128)}) custom-call(bf16[128,8192]{1,0:T(8,128)(2,1)} %li_ref.1, bf16[128,8192]{1,0:T(8,128)(2,1)} %q_ref.1, bf16[128,1024]{1,0:T(8,128)(2,1)} %k_ref.1, bf16[128,8192]{1,0:T(8,128)(2,1)} %go_ref.1, ...), custom_call_target="tpu_custom_call" | custom-call | tf_op jit(solution)/shard_map/packed_backward/pallas_call | solution.py:699
  152.5 0.0 copy-start.2
  152.6 0.0 copy-start
  152.6 3.2 %copy.15 = bf16[128,8192]{1,0:T(8,128)(2,1)} copy(bf16[128,8192]{1,0:T(8,128)(2,1)} %get-tuple-element.8) | data formatting | bytes 4194304
  155.8 0.0 copy-done.2
  155.8 0.7 copy.16
  156.5 0.0 copy-done
  156.5 0.0 copy-start.1
  156.5 1.3 copy.17
  157.8 0.0 copy-done.1
  157.8 0.7 copy.18
Async XLA Ops:
  152.5 3.3 %copy-start.2 = (bf16[128,1024]{1,0:T(8,128)(2,1)S(1)}, bf16[128,1024]{1,0:T(8,128)(2,1)}, u32[]{:S(2)}) copy-start(bf16[128,1024]{1,0:T(8,128)(2,1)} %get-tuple-element.9) | copy-start | bytes 786436
  152.6 4.0 %copy-start = (bf16[128,8192]{1,0:T(8,128)(2,1)S(1)}, bf16[128,8192]{1,0:T(8,128)(2,1)}, u32[]{:S(2)}) copy-start(bf16[128,8192]{1,0:T(8,128)(2,1)} %get-tuple-element.10) | copy-start | bytes 6291460
  156.5 1.3 copy-start.1
